TPU v7x, 32 devices: a whole 2x2x4 slice. The times are simulated.
32 devices in a mesh: grp: 2 (over y), gx: 4 (over z), yz: 4 (over x, core).
Axes of the slice: x: 2, y: 2, z: 4, core: 2. Of those that a mesh axis runs over, the one named last changes fastest.
Arguments:
- rhs: float32 [12, 16, 8, 512], P('gx', 'yz', 'grp'), may hold values from -5 to 5
- coeff: float32 [12, 16, 8], P('gx', 'yz', 'grp'), may hold values from 0.5 to 2
- flags: int32 [12, 16, 8], P('gx', 'yz', 'grp'), may hold values 0 or 1
- basis: float32 [8, 8], replicated, may hold values from -1 to 1, as said below
- eigenvalues: float32 [8], replicated, may hold values from 0.2 to 4
Outputs:
- solution: float32 [12, 16, 8, 512], P('gx', 'yz', 'grp')
Inputs may be any that keep to these rules, and one draw needn't show every extreme that they name: basis is orthogonal: its transpose is its inverse.
All inputs are finite; a program needn't handle non-finite values. No bound on the sum of `flags` on one device may be relied on, other than what follows from the above.
Results may differ from a plain program's by a relative error of at most 0.0003.
Values sent between devices are 32-bit elements; how exact they have to be, the bound alone decides.
A program may use at most 64 MiB of HBM per device.

v0:
```python
import jax
import jax.numpy as jnp
import numpy as np
from jax import lax
from jax.sharding import PartitionSpec as P

DEG1 = 8
ITERS = 2
CHEB = 4


PENALTY = 2.0
COARSE_PENALTY = 1.0
DAMPING = 0.5
CHEB_LOW = 0.1
CHEB_HIGH = 2.0
GLL_POINTS = (
    -1.0,
    -0.8717401485096066,
    -0.5917001814331423,
    -0.2092992179024789,
    0.2092992179024789,
    0.5917001814331423,
    0.8717401485096066,
    1.0,
)
HIGHEST = lax.Precision.HIGHEST


def with_halo(cells, sides, width):
    for axis, dim in sides:
        count = lax.axis_size(axis)
        ends = count - 1
        head = lax.slice_in_dim(cells, 0, width, axis=dim)
        tail = lax.slice_in_dim(cells, cells.shape[dim] - width, cells.shape[dim], axis=dim)
        cells = jnp.concatenate(
            [
                lax.ppermute(tail, axis, [(i, (i + 1) % count) for i in range(ends)]),
                cells,
                lax.ppermute(head, axis, [((i + 1) % count, i) for i in range(ends)]),
            ],
            axis=dim,
        )
    return cells


def build_tables(basis, eigenvalues):
    eigen_table = (
        basis[:, None, None, :, None, None]
        * basis[None, :, None, None, :, None]
        * basis[None, None, :, None, None, :]
    ).reshape(DEG1**3, DEG1**3)
    spectrum = (
        eigenvalues[:, None, None] + eigenvalues[None, :, None] + eigenvalues[None, None, :]
    ).reshape(-1)
    points = jnp.array(np.array(GLL_POINTS), jnp.float32)
    linear = jnp.stack([(1.0 - points) * 0.5, (1.0 + points) * 0.5])
    restrict_table = (
        linear.T[:, None, None, :, None, None]
        * linear.T[None, :, None, None, :, None]
        * linear.T[None, None, :, None, None, :]
    ).reshape(DEG1**3, 8)
    return (eigen_table, spectrum, restrict_table)


def eigen_apply(values, eigen_table, scale):
    flat = values.reshape(-1, eigen_table.shape[0])
    inside = jnp.dot(flat, eigen_table, precision=HIGHEST, preferred_element_type=jnp.float32)
    scaled = inside * scale.reshape(flat.shape)
    back = lax.dot_general(
        scaled,
        eigen_table,
        (((1,), (1,)), ((), ())),
        precision=HIGHEST,
        preferred_element_type=jnp.float32,
    )
    return back.reshape(values.shape)


def boundary_coefs(flag_values, starts, totals, penalty):
    result_list = []
    for dimension in range(3):
        position = starts[dimension] + lax.broadcasted_iota(jnp.int32, flag_values.shape, dimension)
        lower_coef = penalty * jnp.where(position > 0, 1.0, flag_values)
        upper_coef = penalty * jnp.where(position < totals[dimension] - 1, 1.0, flag_values)
        result_list.append((lower_coef[..., None, None, None], upper_coef[..., None, None, None]))
    return result_list


def neighbour_traces(padded, points):
    lower_list, upper_list = ([], [])
    for dimension in range(3):
        interior = [slice(1, -1)] * 3
        before_index = list(interior)
        before_index[dimension] = slice(0, -2)
        after_index = list(interior)
        after_index[dimension] = slice(2, None)
        lower_list.append(
            lax.slice_in_dim(padded[tuple(before_index)], points - 1, points, axis=3 + dimension)
        )
        upper_list.append(lax.slice_in_dim(padded[tuple(after_index)], 0, 1, axis=3 + dimension))
    return (lower_list, upper_list)


def face_term(field, lower_list, upper_list, coefs, penalty):
    summed = jnp.zeros_like(field)
    points = field.shape[3]
    for dimension in range(3):
        node_axis = 3 + dimension
        low_face = lax.slice_in_dim(field, 0, 1, axis=node_axis)
        high_face = lax.slice_in_dim(field, points - 1, points, axis=node_axis)
        lower_coef, upper_coef = coefs[dimension]
        low_term = lower_coef * low_face - penalty * lower_list[dimension]
        high_term = upper_coef * high_face - penalty * upper_list[dimension]
        low_pad = [(0, 0)] * 6
        low_pad[node_axis] = (0, points - 1)
        high_pad = [(0, 0)] * 6
        high_pad[node_axis] = (points - 1, 0)
        summed = summed + jnp.pad(low_term, low_pad) + jnp.pad(high_term, high_pad)
    return summed


def coarse_block(corners, coarse_coeff):
    weight = coarse_coeff[..., None, None, None]
    return weight * (
        3.5 * corners - jnp.flip(corners, 3) - jnp.flip(corners, 4) - jnp.flip(corners, 5)
    )


def chebyshev(coarse_rhs, coarse_coeff, apply_coarse):
    center = 0.5 * (CHEB_HIGH + CHEB_LOW)
    half_width = 0.5 * (CHEB_HIGH - CHEB_LOW)
    sigma_value = center / half_width
    rho_now = 1.0 / sigma_value
    inverse_diag = (1.0 / (coarse_coeff * 3.5 + 3.0 * COARSE_PENALTY))[..., None]
    remain = coarse_rhs
    update = inverse_diag * remain / center
    result = update
    for sweep_num in range(CHEB - 1):
        remain = remain - apply_coarse(update)
        rho_next = 1.0 / (2.0 * sigma_value - rho_now)
        update = rho_next * rho_now * update + 2.0 * rho_next / half_width * (inverse_diag * remain)
        result = result + update
        rho_now = rho_next
    return result


def body(rhs, coeff, flags, basis, eigenvalues):
    eigen_table, spectrum, restrict_table = build_tables(basis, eigenvalues)
    shape_three = rhs.shape[:3]
    node_count = rhs.shape[3]
    flag_values = flags.astype(jnp.float32)
    starts = (
        lax.axis_index("gx") * shape_three[0],
        lax.axis_index("yz") * shape_three[1],
        lax.axis_index("grp") * shape_three[2],
    )
    totals = (
        shape_three[0] * lax.axis_size("gx"),
        shape_three[1] * lax.axis_size("yz"),
        shape_three[2] * lax.axis_size("grp"),
    )
    fine_coefs = boundary_coefs(flag_values, starts, totals, PENALTY)
    block_scale = coeff[..., None] * spectrum
    inverse_scale = 1.0 / block_scale

    def apply_fine(solution):
        field = solution.reshape(shape_three + (DEG1, DEG1, DEG1))
        padded = with_halo(solution, (("gx", 0), ("yz", 1), ("grp", 2)), 1)
        padded = padded.reshape(padded.shape[:3] + (DEG1, DEG1, DEG1))
        lower_list, upper_list = neighbour_traces(padded, DEG1)
        faces = face_term(field, lower_list, upper_list, fine_coefs, PENALTY).reshape(
            solution.shape
        )
        return eigen_apply(solution, eigen_table, block_scale) + faces

    solution = jnp.zeros_like(rhs)
    for iteration in range(ITERS):
        residual = rhs if iteration == 0 else rhs - apply_fine(solution)
        smoothed = eigen_apply(residual, eigen_table, inverse_scale)
        coarse_rhs = jnp.dot(
            residual.reshape(-1, node_count),
            restrict_table,
            precision=HIGHEST,
            preferred_element_type=jnp.float32,
        ).reshape(shape_three + (8,))
        own_coefs = boundary_coefs(flag_values, starts, totals, COARSE_PENALTY)

        def apply_own(values):
            corners = values.reshape(values.shape[:3] + (2, 2, 2))
            padded = with_halo(corners, (("gx", 0), ("yz", 1), ("grp", 2)), 1)
            lower_list, upper_list = neighbour_traces(padded, 2)
            faces = face_term(corners, lower_list, upper_list, own_coefs, COARSE_PENALTY)
            return (coarse_block(corners, coeff) + faces).reshape(values.shape)

        coarse_sol = chebyshev(coarse_rhs, coeff, apply_own)
        lifted = lax.dot_general(
            coarse_sol.reshape(-1, 8),
            restrict_table,
            (((1,), (1,)), ((), ())),
            precision=HIGHEST,
            preferred_element_type=jnp.float32,
        ).reshape(rhs.shape)
        solution = solution + DAMPING * (smoothed + lifted)
    return solution


def solution(mesh):
    in_specs = (P("gx", "yz", "grp", None), P("gx", "yz", "grp"), P("gx", "yz", "grp"), P(), P())
    out_specs = P("gx", "yz", "grp", None)
    return jax.shard_map(body, mesh=mesh, in_specs=in_specs, out_specs=out_specs, check_vma=False)
```

profile of v0, /device:TPU:26, one launch (start us, length us, event | category | flops | bytes accessed | tf_op | source)
XLA Modules:
  0.0 230.2 jit_solution(1724200281067603377)
XLA Ops:
  8.6 8.7 %broadcast_multiply_fusion = f32[8,8,8,8,8,8]{5,4,3,2,1,0:T(8,128)} fusion(f32[8,8]{1,0:T(8,128)} %param.9, f32[8,8,8,8]{3,2,1,0:T(8,128)S(1)} %broadcast_multiply_fusion.2), kind=kLoop, calls=%fused_computation | loop fusion | flops 262144 | bytes 1065216 | tf_op jit(solution)/shard_map/mul | solution.py:49
  18.4 12.6 %mul.684 = f32[512,512]{1,0:T(8,128)S(1)} reshape(f32[8,8,8,8,8,8]{5,4,3,2,1,0:T(8,128)} %broadcast_multiply_fusion) | data formatting | bytes 2097152 | tf_op jit(solution)/shard_map/mul | solution.py:49
  35.7 2.6 %collective-permute-done.2 = f32[5,1,4,2,2,2]{2,5,4,3,1,0:T(2,128)S(1)} collective-permute-done((f32[5,1,4,2,2,2]{2,5,4,3,1,0:T(2,128)S(1)}, f32[5,1,4,2,2,2]{2,5,4,3,1,0:T(2,128)S(1)}, u32[]{:S(2)}, u32[]{:S(2)}) %collective-permute-start.2) | collective-permute-done | bytes 672 | tf_op jit(solution)/shard_map/ppermute | solution.py:38
  38.6 3.4 %collective-permute-start.4 = (f32[5,6,1,2,2,2]{2,5,4,3,1,0:T(2,128)S(1)}, f32[5,6,1,2,2,2]{2,5,4,3,1,0:T(2,128)S(1)}, u32[]{:S(2)}, u32[]{:S(2)}) collective-permute-start(f32[5,6,1,2,2,2]{2,5,4,3,1,0:T(2,128)S(1)} %get-tuple-element.59), channel_id=1, source_target_pairs={{0,16},{1,17},{2,18},{3,19},{4,20},{5,21},{6,22},{7,23},{8,24},{9,... | collective-permute-start | bytes 2888 | tf_op jit(solution)/shard_map/ppermute | solution.py:38
  44.4 4.4 %collective-permute-done.5 = f32[5,6,1,2,2,2]{2,5,4,3,1,0:T(2,128)S(1)} collective-permute-done((f32[5,6,1,2,2,2]{2,5,4,3,1,0:T(2,128)S(1)}, f32[5,6,1,2,2,2]{2,5,4,3,1,0:T(2,128)S(1)}, u32[]{:S(2)}, u32[]{:S(2)}) %collective-permute-start.5) | collective-permute-done | bytes 992 | tf_op jit(solution)/shard_map/ppermute | solution.py:40
  49.6 4.5 %collective-permute-start.7 = (f32[1,4,4,2,2,2]{2,5,4,3,1,0:T(2,128)S(1)}, f32[1,4,4,2,2,2]{2,5,4,3,1,0:T(2,128)S(1)}, u32[]{:S(2)}, u32[]{:S(2)}) collective-permute-start(f32[1,4,4,2,2,2]{2,5,4,3,1,0:T(2,128)S(1)} %bitcast.114), channel_id=1, source_target_pairs={{4,0},{8,4},{12,8},{5,1},{9,5},{13,9},{6,2},{10,6},{14,10},{7,3},{... | collective-permute-start | bytes 1544 | tf_op jit(solution)/shard_map/ppermute | solution.py:40
  56.3 12.6 %reshape.282 = f32[512,512,1,1]{1,0,2,3:T(8,128)S(1)} reshape(f32[8,8,8,8,8,8]{5,4,3,2,1,0:T(8,128)} %broadcast_multiply_fusion) | data formatting | bytes 2097152 | tf_op jit(solution)/shard_map/mul | solution.py:49
  73.5 2.6 %collective-permute-done.8 = f32[5,1,4,2,2,2]{2,5,4,3,1,0:T(2,128)S(1)} collective-permute-done((f32[5,1,4,2,2,2]{2,5,4,3,1,0:T(2,128)S(1)}, f32[5,1,4,2,2,2]{2,5,4,3,1,0:T(2,128)S(1)}, u32[]{:S(2)}, u32[]{:S(2)}) %collective-permute-start.8) | collective-permute-done | bytes 672 | tf_op jit(solution)/shard_map/ppermute | solution.py:38
  80.3 4.4 %collective-permute-done.11 = f32[5,6,1,2,2,2]{2,5,4,3,1,0:T(2,128)S(1)} collective-permute-done((f32[5,6,1,2,2,2]{2,5,4,3,1,0:T(2,128)S(1)}, f32[5,6,1,2,2,2]{2,5,4,3,1,0:T(2,128)S(1)}, u32[]{:S(2)}, u32[]{:S(2)}) %collective-permute-start.11) | collective-permute-done | bytes 992 | tf_op jit(solution)/shard_map/ppermute | solution.py:40
  85.4 4.5 %collective-permute-start.13 = (f32[1,4,4,2,2,2]{2,5,4,3,1,0:T(2,128)S(1)}, f32[1,4,4,2,2,2]{2,5,4,3,1,0:T(2,128)S(1)}, u32[]{:S(2)}, u32[]{:S(2)}) collective-permute-start(f32[1,4,4,2,2,2]{2,5,4,3,1,0:T(2,128)S(1)} %bitcast.111), channel_id=1, source_target_pairs={{4,0},{8,4},{12,8},{5,1},{9,5},{13,9},{6,2},{10,6},{14,10},{7,3},{... | collective-permute-start | bytes 1544 | tf_op jit(solution)/shard_map/ppermute | solution.py:40
  107.0 4.4 %collective-permute-done.17 = f32[5,6,1,2,2,2]{2,5,4,3,1,0:T(2,128)S(1)} collective-permute-done((f32[5,6,1,2,2,2]{2,5,4,3,1,0:T(2,128)S(1)}, f32[5,6,1,2,2,2]{2,5,4,3,1,0:T(2,128)S(1)}, u32[]{:S(2)}, u32[]{:S(2)}) %collective-permute-start.17) | collective-permute-done | bytes 992 | tf_op jit(solution)/shard_map/ppermute | solution.py:40
  116.1 4.2 %collective-permute-done.18 = f32[1,4,4,512]{3,2,1,0:T(4,128)S(1)} collective-permute-done((f32[1,4,4,512]{3,2,1,0:T(4,128)S(1)}, f32[1,4,4,512]{3,2,1,0:T(4,128)S(1)}, u32[]{:S(2)}, u32[]{:S(2)}) %collective-permute-start.18) | collective-permute-done | bytes 32800 | tf_op jit(solution)/shard_map/ppermute | solution.py:38
  124.7 2.9 %collective-permute-done.20 = f32[5,1,4,512]{3,2,1,0:T(4,128)S(1)} collective-permute-done((f32[5,1,4,512]{3,2,1,0:T(4,128)S(1)}, f32[5,1,4,512]{3,2,1,0:T(4,128)S(1)}, u32[]{:S(2)}, u32[]{:S(2)}) %collective-permute-start.20) | collective-permute-done | bytes 40992 | tf_op jit(solution)/shard_map/ppermute | solution.py:38
  129.0 5.8 %collective-permute-start.22 = (f32[5,6,1,512]{3,2,1,0:T(1,128)S(1)}, f32[5,6,1,512]{3,2,1,0:T(1,128)}, u32[]{:S(2)}, u32[]{:S(2)}) collective-permute-start(f32[5,6,1,512]{3,2,1,0:T(1,128)S(1)} %get-tuple-element.33), channel_id=1, source_target_pairs={{0,16},{1,17},{2,18},{3,19},{4,20},{5,21},{6,22},{7,23},{8,24},{9,... | collective-permute-start | bytes 184328 | tf_op jit(solution)/shard_map/ppermute | solution.py:38
  137.5 4.8 %reshape.273 = f32[5,6,6,8,8,8]{5,4,3,2,1,0:T(8,128)} reshape(f32[5,6,6,512]{3,2,1,0:T(8,128)S(1)} %pad_maximum_fusion) | data formatting | bytes 737280 | tf_op jit(solution)/shard_map/reshape | solution.py:170
  142.2 3.0 %fusion.1 = (f32[3,4,4,8,8,1]{5,4,3,2,1,0:T(8,128)S(1)}, f32[3,4,4,8,8,1]{5,4,3,2,1,0:T(8,128)S(1)}) fusion(f32[5,6,6,8,8,8]{5,4,3,2,1,0:T(8,128)} %reshape.273, f32[3,4,4,8,8,8]{5,4,3,2,1,0:T(8,128)S(1)} %reshape.272, f32[3,4,4]{2,1,0:T(4,128)S(1)} %copy-done.7, f32[3,4,4]{2,1,0:T(4,128)S(1)} %copy-done.8), kind=kLoop, calls=%fused_computation.5 | loop fusion | flops 18432 | bytes 74112 | tf_op jit(solution)/shard_map/sub | solution.py:113
  158.7 4.0 %collective-permute-done.24 = f32[1,4,4,2,2,2]{2,5,4,3,1,0:T(2,128)S(1)} collective-permute-done((f32[1,4,4,2,2,2]{2,5,4,3,1,0:T(2,128)S(1)}, f32[1,4,4,2,2,2]{2,5,4,3,1,0:T(2,128)S(1)}, u32[]{:S(2)}, u32[]{:S(2)}) %collective-permute-start.24) | collective-permute-done | bytes 544 | tf_op jit(solution)/shard_map/ppermute | solution.py:38
  167.1 2.6 %collective-permute-done.26 = f32[5,1,4,2,2,2]{2,5,4,3,1,0:T(2,128)S(1)} collective-permute-done((f32[5,1,4,2,2,2]{2,5,4,3,1,0:T(2,128)S(1)}, f32[5,1,4,2,2,2]{2,5,4,3,1,0:T(2,128)S(1)}, u32[]{:S(2)}, u32[]{:S(2)}) %collective-permute-start.26) | collective-permute-done | bytes 672 | tf_op jit(solution)/shard_map/ppermute | solution.py:38
  170.0 4.0 %collective-permute-start.28 = (f32[5,6,1,2,2,2]{2,5,4,3,1,0:T(2,128)S(1)}, f32[5,6,1,2,2,2]{2,5,4,3,1,0:T(2,128)S(1)}, u32[]{:S(2)}, u32[]{:S(2)}) collective-permute-start(f32[5,6,1,2,2,2]{2,5,4,3,1,0:T(2,128)S(1)} %get-tuple-element.47), channel_id=1, source_target_pairs={{0,16},{1,17},{2,18},{3,19},{4,20},{5,21},{6,22},{7,23},{8,24},{9,... | collective-permute-start | bytes 2888 | tf_op jit(solution)/shard_map/ppermute | solution.py:38
  176.4 4.4 %collective-permute-done.29 = f32[5,6,1,2,2,2]{2,5,4,3,1,0:T(2,128)S(1)} collective-permute-done((f32[5,6,1,2,2,2]{2,5,4,3,1,0:T(2,128)S(1)}, f32[5,6,1,2,2,2]{2,5,4,3,1,0:T(2,128)S(1)}, u32[]{:S(2)}, u32[]{:S(2)}) %collective-permute-start.29) | collective-permute-done | bytes 992 | tf_op jit(solution)/shard_map/ppermute | solution.py:40
  185.9 3.3 %collective-permute-done.30 = f32[1,4,4,2,2,2]{2,5,4,3,1,0:T(2,128)S(1)} collective-permute-done((f32[1,4,4,2,2,2]{2,5,4,3,1,0:T(2,128)S(1)}, f32[1,4,4,2,2,2]{2,5,4,3,1,0:T(2,128)S(1)}, u32[]{:S(2)}, u32[]{:S(2)}) %collective-permute-start.30) | collective-permute-done | bytes 544 | tf_op jit(solution)/shard_map/ppermute | solution.py:38
  200.4 4.4 %collective-permute-done.35 = f32[5,6,1,2,2,2]{2,5,4,3,1,0:T(2,128)S(1)} collective-permute-done((f32[5,6,1,2,2,2]{2,5,4,3,1,0:T(2,128)S(1)}, f32[5,6,1,2,2,2]{2,5,4,3,1,0:T(2,128)S(1)}, u32[]{:S(2)}, u32[]{:S(2)}) %collective-permute-start.35) | collective-permute-done | bytes 992 | tf_op jit(solution)/shard_map/ppermute | solution.py:40
  210.2 2.9 %collective-permute-done.36 = f32[1,4,4,2,2,2]{2,5,4,3,1,0:T(2,128)S(1)} collective-permute-done((f32[1,4,4,2,2,2]{2,5,4,3,1,0:T(2,128)S(1)}, f32[1,4,4,2,2,2]{2,5,4,3,1,0:T(2,128)S(1)}, u32[]{:S(2)}, u32[]{:S(2)}) %collective-permute-start.36) | collective-permute-done | bytes 544 | tf_op jit(solution)/shard_map/ppermute | solution.py:38
  224.4 4.4 %collective-permute-done.41 = f32[5,6,1,2,2,2]{2,5,4,3,1,0:T(2,128)S(1)} collective-permute-done((f32[5,6,1,2,2,2]{2,5,4,3,1,0:T(2,128)S(1)}, f32[5,6,1,2,2,2]{2,5,4,3,1,0:T(2,128)S(1)}, u32[]{:S(2)}, u32[]{:S(2)}) %collective-permute-start.41) | collective-permute-done | bytes 992 | tf_op jit(solution)/shard_map/ppermute | solution.py:40
  (223 shorter events, 113.8 us)
Async XLA Ops:
  3.9 27.3 %collective-permute-start.1 = (f32[1,4,4,2,2,2]{2,5,4,3,1,0:T(2,128)S(1)}, f32[1,4,4,2,2,2]{2,5,4,3,1,0:T(2,128)S(1)}, u32[]{:S(2)}, u32[]{:S(2)}) collective-permute-start(f32[1,4,4,2,2,2]{2,5,4,3,1,0:T(2,128)S(1)} %bitcast.109), channel_id=1, source_target_pairs={{4,0},{8,4},{12,8},{5,1},{9,5},{13,9},{6,2},{10,6},{14,10},{7,3},{... | collective-permute-start | bytes 1544 | tf_op jit(solution)/shard_map/ppermute | solution.py:40
  6.3 24.9 %collective-permute-start = (f32[1,4,4,2,2,2]{2,5,4,3,1,0:T(2,128)S(1)}, f32[1,4,4,2,2,2]{2,5,4,3,1,0:T(2,128)S(1)}, u32[]{:S(2)}, u32[]{:S(2)}) collective-permute-start(f32[1,4,4,2,2,2]{2,5,4,3,1,0:T(2,128)S(1)} %bitcast.110), channel_id=1, source_target_pairs={{0,4},{4,8},{8,12},{1,5},{5,9},{9,13},{2,6},{6,10},{10,14},{3,7},{... | collective-permute-start | bytes 1544 | tf_op jit(solution)/shard_map/ppermute | solution.py:38
  33.2 5.1 %collective-permute-start.2 = (f32[5,1,4,2,2,2]{2,5,4,3,1,0:T(2,128)S(1)}, f32[5,1,4,2,2,2]{2,5,4,3,1,0:T(2,128)S(1)}, u32[]{:S(2)}, u32[]{:S(2)}) collective-permute-start(f32[5,1,4,2,2,2]{2,5,4,3,1,0:T(2,128)S(1)} %get-tuple-element.85), channel_id=1, source_target_pairs={{0,1},{1,2},{2,3},{4,5},{5,6},{6,7},{8,9},{9,10},{10,11},{12,13},{... | collective-permute-start | bytes 1928 | tf_op jit(solution)/shard_map/ppermute | solution.py:38
  38.6 5.9 %collective-permute-start.4 = (f32[5,6,1,2,2,2]{2,5,4,3,1,0:T(2,128)S(1)}, f32[5,6,1,2,2,2]{2,5,4,3,1,0:T(2,128)S(1)}, u32[]{:S(2)}, u32[]{:S(2)}) collective-permute-start(f32[5,6,1,2,2,2]{2,5,4,3,1,0:T(2,128)S(1)} %get-tuple-element.59), channel_id=1, source_target_pairs={{0,16},{1,17},{2,18},{3,19},{4,20},{5,21},{6,22},{7,23},{8,24},{9,... | collective-permute-start | bytes 2888 | tf_op jit(solution)/shard_map/ppermute | solution.py:38
  42.0 6.8 %collective-permute-start.5 = (f32[5,6,1,2,2,2]{2,5,4,3,1,0:T(2,128)S(1)}, f32[5,6,1,2,2,2]{2,5,4,3,1,0:T(2,128)S(1)}, u32[]{:S(2)}, u32[]{:S(2)}) collective-permute-start(f32[5,6,1,2,2,2]{2,5,4,3,1,0:T(2,128)S(1)} %get-tuple-element.60), channel_id=1, source_target_pairs={{16,0},{17,1},{18,2},{19,3},{20,4},{21,5},{22,6},{23,7},{24,8},{25... | collective-permute-start | bytes 2888 | tf_op jit(solution)/shard_map/ppermute | solution.py:40
  49.6 19.5 %collective-permute-start.7 = (f32[1,4,4,2,2,2]{2,5,4,3,1,0:T(2,128)S(1)}, f32[1,4,4,2,2,2]{2,5,4,3,1,0:T(2,128)S(1)}, u32[]{:S(2)}, u32[]{:S(2)}) collective-permute-start(f32[1,4,4,2,2,2]{2,5,4,3,1,0:T(2,128)S(1)} %bitcast.114), channel_id=1, source_target_pairs={{4,0},{8,4},{12,8},{5,1},{9,5},{13,9},{6,2},{10,6},{14,10},{7,3},{... | collective-permute-start | bytes 1544 | tf_op jit(solution)/shard_map/ppermute | solution.py:40
  54.2 14.8 %collective-permute-start.6 = (f32[1,4,4,2,2,2]{2,5,4,3,1,0:T(2,128)S(1)}, f32[1,4,4,2,2,2]{2,5,4,3,1,0:T(2,128)S(1)}, u32[]{:S(2)}, u32[]{:S(2)}) collective-permute-start(f32[1,4,4,2,2,2]{2,5,4,3,1,0:T(2,128)S(1)} %bitcast.117), channel_id=1, source_target_pairs={{0,4},{4,8},{8,12},{1,5},{5,9},{9,13},{2,6},{6,10},{10,14},{3,7},{... | collective-permute-start | bytes 1544 | tf_op jit(solution)/shard_map/ppermute | solution.py:38
  71.0 5.1 %collective-permute-start.8 = (f32[5,1,4,2,2,2]{2,5,4,3,1,0:T(2,128)S(1)}, f32[5,1,4,2,2,2]{2,5,4,3,1,0:T(2,128)S(1)}, u32[]{:S(2)}, u32[]{:S(2)}) collective-permute-start(f32[5,1,4,2,2,2]{2,5,4,3,1,0:T(2,128)S(1)} %get-tuple-element.81), channel_id=1, source_target_pairs={{0,1},{1,2},{2,3},{4,5},{5,6},{6,7},{8,9},{9,10},{10,11},{12,13},{... | collective-permute-start | bytes 1928 | tf_op jit(solution)/shard_map/ppermute | solution.py:38
  77.9 6.8 %collective-permute-start.11 = (f32[5,6,1,2,2,2]{2,5,4,3,1,0:T(2,128)S(1)}, f32[5,6,1,2,2,2]{2,5,4,3,1,0:T(2,128)S(1)}, u32[]{:S(2)}, u32[]{:S(2)}) collective-permute-start(f32[5,6,1,2,2,2]{2,5,4,3,1,0:T(2,128)S(1)} %get-tuple-element.56), channel_id=1, source_target_pairs={{16,0},{17,1},{18,2},{19,3},{20,4},{21,5},{22,6},{23,7},{24,8},{25... | collective-permute-start | bytes 2888 | tf_op jit(solution)/shard_map/ppermute | solution.py:40
  85.4 7.7 %collective-permute-start.13 = (f32[1,4,4,2,2,2]{2,5,4,3,1,0:T(2,128)S(1)}, f32[1,4,4,2,2,2]{2,5,4,3,1,0:T(2,128)S(1)}, u32[]{:S(2)}, u32[]{:S(2)}) collective-permute-start(f32[1,4,4,2,2,2]{2,5,4,3,1,0:T(2,128)S(1)} %bitcast.111), channel_id=1, source_target_pairs={{4,0},{8,4},{12,8},{5,1},{9,5},{13,9},{6,2},{10,6},{14,10},{7,3},{... | collective-permute-start | bytes 1544 | tf_op jit(solution)/shard_map/ppermute | solution.py:40
  90.1 5.6 %collective-permute-start.12 = (f32[1,4,4,2,2,2]{2,5,4,3,1,0:T(2,128)S(1)}, f32[1,4,4,2,2,2]{2,5,4,3,1,0:T(2,128)S(1)}, u32[]{:S(2)}, u32[]{:S(2)}) collective-permute-start(f32[1,4,4,2,2,2]{2,5,4,3,1,0:T(2,128)S(1)} %bitcast.112), channel_id=1, source_target_pairs={{0,4},{4,8},{8,12},{1,5},{5,9},{9,13},{2,6},{6,10},{10,14},{3,7},{... | collective-permute-start | bytes 1544 | tf_op jit(solution)/shard_map/ppermute | solution.py:38
  97.7 5.1 %collective-permute-start.14 = (f32[5,1,4,2,2,2]{2,5,4,3,1,0:T(2,128)S(1)}, f32[5,1,4,2,2,2]{2,5,4,3,1,0:T(2,128)S(1)}, u32[]{:S(2)}, u32[]{:S(2)}) collective-permute-start(f32[5,1,4,2,2,2]{2,5,4,3,1,0:T(2,128)S(1)} %get-tuple-element.77), channel_id=1, source_target_pairs={{0,1},{1,2},{2,3},{4,5},{5,6},{6,7},{8,9},{9,10},{10,11},{12,13},{... | collective-permute-start | bytes 1928 | tf_op jit(solution)/shard_map/ppermute | solution.py:38
  104.5 6.8 %collective-permute-start.17 = (f32[5,6,1,2,2,2]{2,5,4,3,1,0:T(2,128)S(1)}, f32[5,6,1,2,2,2]{2,5,4,3,1,0:T(2,128)S(1)}, u32[]{:S(2)}, u32[]{:S(2)}) collective-permute-start(f32[5,6,1,2,2,2]{2,5,4,3,1,0:T(2,128)S(1)} %get-tuple-element.52), channel_id=1, source_target_pairs={{16,0},{17,1},{18,2},{19,3},{20,4},{21,5},{22,6},{23,7},{24,8},{25... | collective-permute-start | bytes 2888 | tf_op jit(solution)/shard_map/ppermute | solution.py:40
  114.5 5.8 %collective-permute-start.18 = (f32[1,4,4,512]{3,2,1,0:T(4,128)S(1)}, f32[1,4,4,512]{3,2,1,0:T(4,128)S(1)}, u32[]{:S(2)}, u32[]{:S(2)}) collective-permute-start(f32[1,4,4,512]{3,2,1,0:T(4,128)S(1)} %get-tuple-element.61), channel_id=1, source_target_pairs={{0,4},{4,8},{8,12},{1,5},{5,9},{9,13},{2,6},{6,10},{10,14},{3,7},{... | collective-permute-start | bytes 98312 | tf_op jit(solution)/shard_map/ppermute | solution.py:38
  122.3 5.3 %collective-permute-start.20 = (f32[5,1,4,512]{3,2,1,0:T(4,128)S(1)}, f32[5,1,4,512]{3,2,1,0:T(4,128)S(1)}, u32[]{:S(2)}, u32[]{:S(2)}) collective-permute-start(f32[5,1,4,512]{3,2,1,0:T(4,128)S(1)} %get-tuple-element.35), channel_id=1, source_target_pairs={{0,1},{1,2},{2,3},{4,5},{5,6},{6,7},{8,9},{9,10},{10,11},{12,13},{... | collective-permute-start | bytes 122888 | tf_op jit(solution)/shard_map/ppermute | solution.py:38
  127.7 8.7 %collective-permute-start.23 = (f32[5,6,1,512]{3,2,1,0:T(1,128)S(1)}, f32[5,6,1,512]{3,2,1,0:T(1,128)}, u32[]{:S(2)}, u32[]{:S(2)}) collective-permute-start(f32[5,6,1,512]{3,2,1,0:T(1,128)S(1)} %get-tuple-element.34), channel_id=1, source_target_pairs={{16,0},{17,1},{18,2},{19,3},{20,4},{21,5},{22,6},{23,7},{24,8},{25... | collective-permute-start | bytes 184328 | tf_op jit(solution)/shard_map/ppermute | solution.py:40
  129.0 7.4 %collective-permute-start.22 = (f32[5,6,1,512]{3,2,1,0:T(1,128)S(1)}, f32[5,6,1,512]{3,2,1,0:T(1,128)}, u32[]{:S(2)}, u32[]{:S(2)}) collective-permute-start(f32[5,6,1,512]{3,2,1,0:T(1,128)S(1)} %get-tuple-element.33), channel_id=1, source_target_pairs={{0,16},{1,17},{2,18},{3,19},{4,20},{5,21},{6,22},{7,23},{8,24},{9,... | collective-permute-start | bytes 184328 | tf_op jit(solution)/shard_map/ppermute | solution.py:38
  157.1 5.6 %collective-permute-start.24 = (f32[1,4,4,2,2,2]{2,5,4,3,1,0:T(2,128)S(1)}, f32[1,4,4,2,2,2]{2,5,4,3,1,0:T(2,128)S(1)}, u32[]{:S(2)}, u32[]{:S(2)}) collective-permute-start(f32[1,4,4,2,2,2]{2,5,4,3,1,0:T(2,128)S(1)} %bitcast.120), channel_id=1, source_target_pairs={{0,4},{4,8},{8,12},{1,5},{5,9},{9,13},{2,6},{6,10},{10,14},{3,7},{... | collective-permute-start | bytes 1544 | tf_op jit(solution)/shard_map/ppermute | solution.py:38
  170.0 6.4 %collective-permute-start.28 = (f32[5,6,1,2,2,2]{2,5,4,3,1,0:T(2,128)S(1)}, f32[5,6,1,2,2,2]{2,5,4,3,1,0:T(2,128)S(1)}, u32[]{:S(2)}, u32[]{:S(2)}) collective-permute-start(f32[5,6,1,2,2,2]{2,5,4,3,1,0:T(2,128)S(1)} %get-tuple-element.47), channel_id=1, source_target_pairs={{0,16},{1,17},{2,18},{3,19},{4,20},{5,21},{6,22},{7,23},{8,24},{9,... | collective-permute-start | bytes 2888 | tf_op jit(solution)/shard_map/ppermute | solution.py:38
  174.0 6.8 %collective-permute-start.29 = (f32[5,6,1,2,2,2]{2,5,4,3,1,0:T(2,128)S(1)}, f32[5,6,1,2,2,2]{2,5,4,3,1,0:T(2,128)S(1)}, u32[]{:S(2)}, u32[]{:S(2)}) collective-permute-start(f32[5,6,1,2,2,2]{2,5,4,3,1,0:T(2,128)S(1)} %get-tuple-element.48), channel_id=1, source_target_pairs={{16,0},{17,1},{18,2},{19,3},{20,4},{21,5},{22,6},{23,7},{24,8},{25... | collective-permute-start | bytes 2888 | tf_op jit(solution)/shard_map/ppermute | solution.py:40
  183.6 5.6 %collective-permute-start.30 = (f32[1,4,4,2,2,2]{2,5,4,3,1,0:T(2,128)S(1)}, f32[1,4,4,2,2,2]{2,5,4,3,1,0:T(2,128)S(1)}, u32[]{:S(2)}, u32[]{:S(2)}) collective-permute-start(f32[1,4,4,2,2,2]{2,5,4,3,1,0:T(2,128)S(1)} %bitcast.115), channel_id=1, source_target_pairs={{0,4},{4,8},{8,12},{1,5},{5,9},{9,13},{2,6},{6,10},{10,14},{3,7},{... | collective-permute-start | bytes 1544 | tf_op jit(solution)/shard_map/ppermute | solution.py:38
  198.0 6.8 %collective-permute-start.35 = (f32[5,6,1,2,2,2]{2,5,4,3,1,0:T(2,128)S(1)}, f32[5,6,1,2,2,2]{2,5,4,3,1,0:T(2,128)S(1)}, u32[]{:S(2)}, u32[]{:S(2)}) collective-permute-start(f32[5,6,1,2,2,2]{2,5,4,3,1,0:T(2,128)S(1)} %get-tuple-element.44), channel_id=1, source_target_pairs={{16,0},{17,1},{18,2},{19,3},{20,4},{21,5},{22,6},{23,7},{24,8},{25... | collective-permute-start | bytes 2888 | tf_op jit(solution)/shard_map/ppermute | solution.py:40
  207.5 5.6 %collective-permute-start.36 = (f32[1,4,4,2,2,2]{2,5,4,3,1,0:T(2,128)S(1)}, f32[1,4,4,2,2,2]{2,5,4,3,1,0:T(2,128)S(1)}, u32[]{:S(2)}, u32[]{:S(2)}) collective-permute-start(f32[1,4,4,2,2,2]{2,5,4,3,1,0:T(2,128)S(1)} %bitcast.119), channel_id=1, source_target_pairs={{0,4},{4,8},{8,12},{1,5},{5,9},{9,13},{2,6},{6,10},{10,14},{3,7},{... | collective-permute-start | bytes 1544 | tf_op jit(solution)/shard_map/ppermute | solution.py:38
  222.0 6.8 %collective-permute-start.41 = (f32[5,6,1,2,2,2]{2,5,4,3,1,0:T(2,128)S(1)}, f32[5,6,1,2,2,2]{2,5,4,3,1,0:T(2,128)S(1)}, u32[]{:S(2)}, u32[]{:S(2)}) collective-permute-start(f32[5,6,1,2,2,2]{2,5,4,3,1,0:T(2,128)S(1)} %get-tuple-element.40), channel_id=1, source_target_pairs={{16,0},{17,1},{18,2},{19,3},{20,4},{21,5},{22,6},{23,7},{24,8},{25... | collective-permute-start | bytes 2888 | tf_op jit(solution)/shard_map/ppermute | solution.py:40
  (32 other events, 258.0 us)
where the time goes:
time: 232 us; the launch traced here: 230 us
  starting transfers between devices  87.4 us (38%)
  waiting for transfers between devices  68.5 us (30%)
  local copies, waits for them, and re-layouts  39.6 us (17%)
  other arithmetic  26.1 us (11%)
  matrix products  7.29 us (3%)
    ppermute x21, starting transfers between devices, with_halo(): lax.ppermute(tail, axis, [(i, (i + 1) % count) for i in range(ends)])  45 us
    ppermute x21, starting transfers between devices, with_halo(): lax.ppermute(head, axis, [((i + 1) % count, i) for i in range(ends)])  42.5 us
    ppermute x21, waiting for transfers between devices, with_halo(): lax.ppermute(tail, axis, [(i, (i + 1) % count) for i in range(ends)])  42.1 us
    ppermute x21, waiting for transfers between devices, with_halo(): lax.ppermute(head, axis, [((i + 1) % count, i) for i in range(ends)])  26.4 us
    mul x2, local copies, waits for them, and re-layouts, build_tables(): basis[:, None, None, :, None, None] * basis[None, :, None, None, :, None]  25.2 us
    mul x2, other arithmetic, build_tables(): basis[:, None, None, :, None, None] * basis[None, :, None, None, :, None]  9.6 us
    sub x21, other arithmetic, face_term(): low_term = lower_coef * low_face - penalty * lower_list[dimension]  8.43 us
    reshape x1, local copies, waits for them, and re-layouts, apply_fine(): padded = padded.reshape(padded.shape[:3] + (DEG1, DEG1, DEG1))  4.77 us
  transfers between devices with their start and end apart: 42, of which 25 were waited for; matrix products, arithmetic and copies ran while one was open for 19% of the time, Pallas kernels for 0%

commit v1 on v0

v1 whole, which is shorter than its diff:
```python
import functools

import jax
import jax.numpy as jnp
import numpy as np
from jax import lax
from jax.experimental import pallas as pl
from jax.experimental.pallas import tpu as pltpu
from jax.sharding import PartitionSpec as P

DEG1 = 8
NODES = 512
CHEB = 4
CHEB_LOW = 0.1
CHEB_HIGH = 2.0
REACH = 7
REACH_FACE = 4
GLL_POINTS = (
    -1.0,
    -0.8717401485096066,
    -0.5917001814331423,
    -0.2092992179024789,
    0.2092992179024789,
    0.5917001814331423,
    0.8717401485096066,
    1.0,
)
L0 = [(1.0 - x) * 0.5 for x in GLL_POINTS]
L1 = [(1.0 + x) * 0.5 for x in GLL_POINTS]
MASS_SAME = sum(a * a for a in L0)
MASS_OTHER = sum(a * b for a, b in zip(L0, L1))
HIGHEST = lax.Precision.HIGHEST
MESH = pl.DeviceIdType.MESH
F32 = jnp.float32
BF16 = jnp.bfloat16


def iota(shape, dim):
    return lax.broadcasted_iota(jnp.int32, shape, dim)


def dot(a, b, dims=((1,), (0,))):
    return lax.dot_general(a, b, (dims, ((), ())), precision=HIGHEST, preferred_element_type=F32)


def split(x):
    hi = x.astype(BF16)
    return hi, (x - hi.astype(F32)).astype(BF16)


def dot3(x, hi, lo):
    xh, xl = split(x)
    d = functools.partial(jnp.dot, preferred_element_type=F32)
    return d(xh, hi) + (d(xl, hi) + d(xh, lo))


def pick(index, table):
    out = jnp.full(index.shape, table[0], F32)
    for i in range(1, len(table)):
        out = jnp.where(index == i, table[i], out)
    return out


def offsets(reach):
    return [k for r in range(1, reach + 1) for k in (-r, r)]


def kernel(
    cfg,
    rhs_ref, coeff_ref, flags_ref, basis_ref, eig_ref,
    out_ref,
    mine, other, win, planes, cfx, ext3, ext1,
    rhs_s, s_ref, e_hi, e_lo, t_hi, t_lo,
    ysend, yrecv, zsend, zrecv, xrecv, nb,
    send_sem, recv_sem, fsend, frecv,
):
    n_grp, n_gx, n_yz, LX, LY, LZ, WG, WH, RG, RH, RGF, RHF = cfg
    LT = planes.shape[0]
    L = LT * 128
    XP = cfx.shape[1]
    FROWS = XP * 8
    me_grp = lax.axis_index("grp")
    me_gx = lax.axis_index("gx")
    me_yz = lax.axis_index("yz")
    full_g = WG == n_gx
    full_h = WH == n_yz
    gs = me_gx if full_g else RG
    hs = me_yz if full_h else RH
    g_start = 0 if full_g else me_gx - RG
    h_start = 0 if full_h else me_yz - RH

    win[...] = jnp.zeros(win.shape, F32)
    planes[...] = jnp.zeros(planes.shape, F32)
    cfx[...] = jnp.zeros(cfx.shape, F32)

    me_of = {"grp": me_grp, "gx": me_gx, "yz": me_yz}
    n_of = {"grp": n_grp, "gx": n_gx, "yz": n_yz}

    def exists(axis, k):
        at = me_of[axis] + k
        return jnp.logical_and(at >= 0, at < n_of[axis])

    peers = [("grp", k) for k in offsets(min(1, n_grp - 1))]
    peers += [("gx", k) for k in offsets(RG)]
    peers += [("yz", k) for k in offsets(RH)]

    barrier = pltpu.get_barrier_semaphore()
    count = jnp.int32(0)
    for axis, k in peers:
        here = exists(axis, k)
        count = count + here.astype(jnp.int32)

        @pl.when(here)
        def _(axis=axis, k=k):
            pl.semaphore_signal(barrier, inc=1, device_id={axis: me_of[axis] + k}, device_id_type=MESH)

    basis = basis_ref[...]
    lane = iota((8, NODES), 1)
    sub = iota((8, NODES), 0)
    v1 = (lane // 64 == sub).astype(F32)
    v2 = ((lane // 8) % 8 == sub).astype(F32)
    v3 = (lane % 8 == sub).astype(F32)

    def build(hi_ref, lo_ref, dims):
        t1 = dot(basis, v1, dims)
        t2 = dot(basis, v2, dims)
        t3 = dot(basis, v3, dims)
        pairs = jnp.concatenate([t2[j : j + 1, :] * t3 for j in range(8)], axis=0)
        for i in range(8):
            hi, lo = split(t1[i : i + 1, :] * pairs)
            hi_ref[i * 64 : (i + 1) * 64, :] = hi
            lo_ref[i * 64 : (i + 1) * 64, :] = lo

    build(e_hi, e_lo, ((1,), (0,)))
    build(t_hi, t_lo, ((0,), (0,)))
    spectrum = dot(eig_ref[...], v1 + v2 + v3)

    node_at = (lane // 64, (lane // 8) % 8, lane % 8)
    side_at = (sub // 4, (sub // 2) % 2, sub % 2)
    restrict = jnp.ones((8, NODES), F32)
    for d in range(3):
        restrict = restrict * jnp.where(side_at[d] == 0, pick(node_at[d], L0), pick(node_at[d], L1))
    on_face = [
        jnp.where(node_at[d] == 7 * side_at[d], restrict, 0.0) for d in range(3)
    ]
    faces = jnp.concatenate(on_face, axis=0)

    YZ = LY * LZ
    NE = LX * YZ
    for x in range(LX):
        for y in range(LY):
            at = x * YZ + y * LZ
            rhs_s[at : at + LZ, :] = rhs_ref[x, y]
    rhs = rhs_s[...]
    row = iota((NE, 1), 0)
    row_x, row_y, row_z = row // YZ, (row // LZ) % LY, row % LZ
    ysel = (iota((YZ, LY), 0) // LZ == iota((YZ, LY), 1)).astype(F32)
    zsel = iota((YZ, LZ), 0) % LZ == iota((YZ, LZ), 1)

    def column(ref):
        parts = []
        for x in range(LX):
            spread = dot(ysel, ref[x].astype(F32))
            parts.append(jnp.sum(jnp.where(zsel, spread, 0.0), axis=1, keepdims=True))
        return parts

    coeff_cols = column(coeff_ref)
    flag_cols = column(flags_ref)
    coeff_col = jnp.concatenate(coeff_cols, axis=0)
    flag_col = jnp.concatenate(flag_cols, axis=0)
    inverse = 1.0 / (coeff_col * spectrum)

    r16 = iota((YZ, 128), 0)
    l16 = iota((YZ, 128), 1)
    spot = (r16 // LZ) * 8 + me_grp * LZ + r16 % LZ
    tail = (l16 == 96 + spot).astype(F32)
    re = iota((NE, 128), 0)
    place = (
        iota((NE, 128), 1) == (re // YZ) * 32 + ((re // LZ) % LY) * 8 + me_grp * LZ + re % LZ
    ).astype(F32)

    b_own = dot(dot(restrict, rhs, ((1,), (1,))), place)
    row8 = iota((8, 128), 0)
    for x in range(LX):
        c_line = jnp.sum(coeff_cols[x] * tail, axis=0, keepdims=True)
        f_line = jnp.sum(flag_cols[x] * tail, axis=0, keepdims=True)
        b_own = b_own + jnp.where(row8 == x, c_line, 0.0) + jnp.where(row8 == LX + x, f_line, 0.0)
    s = dot3(dot3(rhs, e_hi[...], e_lo[...]) * inverse, t_hi[...], t_lo[...])
    s_ref[...] = s
    mine[0:8, :] = b_own
    mine[8:32, :] = dot(dot(faces, s, ((1,), (1,))), place)

    for side in range(2):
        yy, zz = (0, 0) if side == 0 else (LY - 1, LZ - 1)
        for x in range(LX):
            ysend[side, x * LZ : (x + 1) * LZ, :] = s_ref[x * YZ + yy * LZ : x * YZ + (yy + 1) * LZ, :]
            for y in range(LY):
                at = x * YZ + y * LZ + zz
                zsend[side, x * LY + y : x * LY + y + 1, :] = s_ref[at : at + 1, :]

    def face_copies():
        found = []
        for n, (axis, k) in enumerate(
            [("gx", -1), ("gx", 1), ("yz", -1), ("yz", 1), ("grp", -1), ("grp", 1)]
        ):
            if n_of[axis] == 1:
                continue
            side = 0 if k < 0 else 1
            if axis == "gx":
                at = 0 if side == 0 else (LX - 1) * YZ
                src, dst = s_ref.at[pl.ds(at, YZ)], xrecv.at[1 - side]
            elif axis == "yz":
                src, dst = ysend.at[side], yrecv.at[1 - side]
            else:
                src, dst = zsend.at[side], zrecv.at[1 - side]
            copy = pltpu.make_async_remote_copy(
                src_ref=src, dst_ref=dst, send_sem=fsend.at[n], recv_sem=frecv.at[n],
                device_id={axis: me_of[axis] + k}, device_id_type=MESH,
            )
            found.append((axis, k, copy))
        return found

    def phase_copies(axis):
        found = []
        for axis_p, k in peers:
            n = peers.index((axis_p, k))
            if axis_p != axis:
                continue
            if axis == "grp":
                src, dst = mine, other
            elif axis == "gx":
                src, dst = win.at[hs, gs], win.at[hs, gs if full_g else RG - k]
                if abs(k) > RGF:
                    src, dst = src.at[pl.ds(0, 8)], dst.at[pl.ds(0, 8)]
            else:
                src, dst = win.at[hs], win.at[hs if full_h else RH - k]
                if abs(k) > RHF:
                    src, dst = src.at[:, pl.ds(0, 8)], dst.at[:, pl.ds(0, 8)]
            copy = pltpu.make_async_remote_copy(
                src_ref=src, dst_ref=dst, send_sem=send_sem.at[n], recv_sem=recv_sem.at[n],
                device_id={axis: me_of[axis] + k}, device_id_type=MESH,
            )
            found.append((axis, k, copy))
        return found

    def recv_of(axis, k, copy_list):
        return next(c for a, j, c in copy_list if (a, j) == (axis, k))

    def start_all(copies):
        for axis, k, copy in copies:
            @pl.when(exists(axis, k))
            def _(copy=copy):
                copy.start()

    def wait_recv(copies):
        for axis, k, copy in copies:
            @pl.when(exists(axis, -k))
            def _(copy=copy):
                copy.wait_recv()

    def wait_send(copies):
        for axis, k, copy in copies:
            @pl.when(exists(axis, k))
            def _(copy=copy):
                copy.wait_send()

    pl.semaphore_wait(barrier, count)

    grp_copies = phase_copies("grp")
    gx_copies = phase_copies("gx")
    yz_copies = phase_copies("yz")
    next_door = face_copies()
    start_all(grp_copies)
    wait_recv(grp_copies)
    if n_grp > 1:
        win[hs, gs] = mine[...] + other[...]
    else:
        win[hs, gs] = mine[...]
    start_all(gx_copies)
    start_all(next_door)
    wait_recv(gx_copies)
    start_all(yz_copies)
    wait_recv(next_door)

    own_at = (me_gx * LX + row_x, me_yz * LY + row_y, me_grp * LZ + row_z)
    totals = (n_gx * LX, n_yz * LY, n_grp * LZ)
    node_lane = iota((1, NODES), 1)
    node_of = (node_lane // 64, (node_lane // 8) % 8, node_lane % 8)
    strides = (64, 8, 1)
    face_s = jnp.zeros((NE, NODES), F32)
    for d in range(3):
        for side in range(2):
            if d == 0:
                if side == 0:
                    beside = jnp.concatenate([xrecv[0], s[: NE - YZ]], axis=0)
                else:
                    beside = jnp.concatenate([s[YZ:], xrecv[1]], axis=0)
            else:
                step = LZ if d == 1 else 1
                nb[...] = pltpu.roll(s, step if side == 0 else NE - step, 0)
                for x in range(LX):
                    if d == 1:
                        at = x * YZ + (0 if side == 0 else (LY - 1) * LZ)
                        nb[at : at + LZ, :] = yrecv[side, x * LZ : (x + 1) * LZ, :]
                    else:
                        for y in range(LY):
                            at = x * YZ + y * LZ + (0 if side == 0 else LZ - 1)
                            nb[at : at + 1, :] = zrecv[side, x * LY + y : x * LY + y + 1, :]
                beside = nb[...]
            has = own_at[d] > 0 if side == 0 else own_at[d] < totals[d] - 1
            gain = jnp.where(has, 1.0, flag_col)
            shift = 7 * strides[d]
            moved = pltpu.roll(beside, NODES - shift if side == 0 else shift, 1)
            term = gain * s - jnp.where(has, moved, 0.0)
            face_s = face_s + jnp.where(node_of[d] == 7 * side, term, 0.0)

    wait_recv(yz_copies)

    lane_slot = iota((32, L), 1) // 32
    for g in range(WG):
        cf_plane = jnp.zeros((8, L), F32)
        tiles = []
        for h in range(WH):
            tile = win[h, g]
            if L > 128:
                tile = jnp.concatenate([tile, jnp.zeros((32, L - 128), F32)], axis=1)
            tiles.append(tile)
            moved = pltpu.roll(tile[0:8], (32 * (h - 3)) % L, 1)
            cf_plane = jnp.where(lane_slot[0:8] == h, moved, cf_plane)
        for x in range(LX):
            plane = jnp.zeros((32, L), F32)
            for h in range(WH):
                amount = (32 * (h - x)) % L
                moved = pltpu.roll(tiles[h], amount, 1) if amount else tiles[h]
                plane = jnp.where(lane_slot == h, moved, plane)
            at = (g * LX + x) * 8
            for f in range(4):
                for t in range(LT):
                    part = plane[f * 8 : f * 8 + 8, t * 128 : (t + 1) * 128]
                    planes[t, f * FROWS + at : f * FROWS + at + 8, :] = part
        cfx[0, g * LX : (g + 1) * LX, :] = cf_plane[0:LX]
        cfx[1, g * LX : (g + 1) * LX, :] = cf_plane[LX : 2 * LX]

    def strided(ref, start, stride):
        parts = [ref[t, pl.ds(start, XP, stride=stride), :] for t in range(LT)]
        return parts[0] if LT == 1 else jnp.concatenate(parts, axis=1)

    def store_strided(ref, start, stride, value):
        for t in range(LT):
            ref[t, pl.ds(start, XP, stride=stride), :] = value[:, t * 128 : (t + 1) * 128]

    def field(f):
        return [strided(planes, f * FROWS + a, 8) for a in range(8)]

    rhs1 = field(0)
    proj = [field(1 + d) for d in range(3)]
    coeff = cfx[0]
    flag = cfx[1]
    pos = (
        g_start * LX + iota((XP, L), 0),
        h_start * LY + iota((XP, L), 1) // 8,
        iota((XP, L), 1) % 8,
    )
    has = [(pos[d] > 0, pos[d] < totals[d] - 1) for d in range(3)]
    gain = [[jnp.where(has[d][q], 1.0, flag) for q in range(2)] for d in range(3)]
    roll_axis = (0, 1, 1)
    roll_step = (1, 8, 1)
    bit = (4, 2, 1)

    def side_of(a, d):
        return (a // bit[d]) % 2

    def beside_of(v, a, d):
        q = side_of(a, d)
        size = XP if d == 0 else L
        step = roll_step[d] if q == 0 else size - roll_step[d]
        return jnp.where(has[d][q], pltpu.roll(v[a ^ bit[d]], step, roll_axis[d]), 0.0)

    def jump(v, a, d):
        return gain[d][side_of(a, d)] * v[a] - beside_of(v, a, d)

    diag = [
        coeff * 3.5 + gain[0][side_of(a, 0)] + gain[1][side_of(a, 1)] + gain[2][side_of(a, 2)]
        for a in range(8)
    ]

    def coarse_apply(v):
        out = []
        for a in range(8):
            flips = v[a ^ 4] + v[a ^ 2] + v[a ^ 1]
            sides = beside_of(v, a, 0) + beside_of(v, a, 1) + beside_of(v, a, 2)
            out.append(diag[a] * v[a] - coeff * flips - sides)
        return out

    center = 0.5 * (CHEB_HIGH + CHEB_LOW)
    half_width = 0.5 * (CHEB_HIGH - CHEB_LOW)
    inverse_diag = 1.0 / (coeff * 3.5 + 3.0)

    def cheb(f):
        sigma = center / half_width
        rho = 1.0 / sigma
        remain = f
        first = inverse_diag * (1.0 / center)
        update = [first * r for r in remain]
        result = update
        for _ in range(CHEB - 1):
            applied = coarse_apply(update)
            remain = [r - t for r, t in zip(remain, applied)]
            rho_next = 1.0 / (2.0 * sigma - rho)
            weight = inverse_diag * (2.0 * rho_next / half_width)
            update = [(rho_next * rho) * u + weight * r for u, r in zip(update, remain)]
            result = [t + u for t, u in zip(result, update)]
            rho = rho_next
        return result

    col = iota((8, 8), 0)
    w = [jnp.sum(pick(col, t) * basis, axis=0, keepdims=True) for t in (L0, L1)]
    eig = eig_ref[...]
    stiff = [[jnp.sum(eig * w[p] * w[q], axis=1, keepdims=True) for q in range(2)] for p in range(2)]

    def mass(v, d):
        return [MASS_SAME * v[a] + MASS_OTHER * v[a ^ bit[d]] for a in range(8)]

    c1 = cheb(rhs1)
    m3 = mass(c1, 2)
    m23 = mass(m3, 1)
    m13 = mass(m3, 0)
    m12 = mass(mass(c1, 1), 0)
    masses = (m23, m13, m12)
    rhs2 = []
    for a in range(8):
        inner = 0.0
        for d in range(3):
            q = side_of(a, d)
            inner = inner + stiff[q][q] * masses[d][a] + stiff[q][1 - q] * masses[d][a ^ bit[d]]
        rhs2.append(0.5 * rhs1[a] - 0.5 * coeff * inner)
    for d in range(3):
        both = [proj[d][a] + masses[d][a] for a in range(8)]
        rhs2 = [rhs2[a] - jump(both, a, d) for a in range(8)]

    first_row = gs * LX
    absolute = hs * 32 + (iota((YZ, L), 0) // LZ) * 8 + me_grp * LZ + iota((YZ, L), 0) % LZ
    take = (iota((YZ, L), 1) == absolute).astype(F32)

    def own_values(ref, comps):
        parts = []
        for x in range(LX):
            start = pl.multiple_of((first_row + x) * comps, 8)
            part = 0.0
            for t in range(LT):
                lanes = take[:, t * 128 : (t + 1) * 128]
                part = part + dot(lanes, ref[t, pl.ds(start, comps), :], ((1,), (1,)))
            parts.append(part)
        return jnp.concatenate(parts, axis=0)

    for d in range(3):
        for a in range(8):
            store_strided(ext3, d * 8 + a, 24, jump(c1, a, d))
    face_c = dot(own_values(ext3, 24), faces)
    total = face_s + face_c
    smooth2 = dot3(dot3(total, e_hi[...], e_lo[...]) * inverse, t_hi[...], t_lo[...])

    c2 = cheb(rhs2)
    for a in range(8):
        store_strided(ext1, a, 8, 0.25 * c1[a] + 0.5 * c2[a])
    lifted = dot(own_values(ext1, 8), restrict)
    out_ref[...] = 0.75 * s + lifted - 0.5 * smooth2

    for copies in (grp_copies, gx_copies, yz_copies, next_door):
        wait_send(copies)


def body(cfg, rhs, coeff, flags, basis, eigenvalues):
    n_grp, n_gx, n_yz, LX, LY, LZ, WG, WH, RG, RH, RGF, RHF = cfg
    NE = LX * LY * LZ
    L = -(-(WH * 32) // 128) * 128
    XP = -(-(WG * LX) // 8) * 8
    V = pltpu.VMEM
    n_peers = 2 * (1 + RG + RH)
    out = pl.pallas_call(
        functools.partial(kernel, cfg),
        out_shape=jax.ShapeDtypeStruct((NE, NODES), F32),
        in_specs=[pl.BlockSpec(memory_space=V)] * 5,
        out_specs=pl.BlockSpec(memory_space=V),
        scratch_shapes=[
            V((32, 128), F32),
            V((32, 128), F32),
            V((WH, WG, 32, 128), F32),
            V((L // 128, 4 * XP * 8, 128), F32),
            V((2, XP, L), F32),
            V((L // 128, XP * 24, 128), F32),
            V((L // 128, XP * 8, 128), F32),
            V((NE, NODES), F32),
            V((NE, NODES), F32),
            V((NODES, NODES), BF16),
            V((NODES, NODES), BF16),
            V((NODES, NODES), BF16),
            V((NODES, NODES), BF16),
            V((2, 16, NODES), F32),
            V((2, 16, NODES), F32),
            V((2, 16, NODES), F32),
            V((2, 16, NODES), F32),
            V((2, LY * LZ, NODES), F32),
            V((NE, NODES), F32),
            pltpu.SemaphoreType.DMA((n_peers,)),
            pltpu.SemaphoreType.DMA((n_peers,)),
            pltpu.SemaphoreType.DMA((6,)),
            pltpu.SemaphoreType.DMA((6,)),
        ],
        compiler_params=pltpu.CompilerParams(
            collective_id=0, has_side_effects=True, vmem_limit_bytes=32 * 1024 * 1024
        ),
    )(rhs, coeff, flags, basis, eigenvalues.reshape(1, DEG1))
    return out.reshape(rhs.shape)


def solution(mesh):
    n_grp, n_gx, n_yz = (mesh.shape[a] for a in ("grp", "gx", "yz"))

    def call(rhs, coeff, flags, basis, eigenvalues):
        EX, EY, EZ = rhs.shape[:3]
        LX, LY, LZ = EX // n_gx, EY // n_yz, EZ // n_grp
        assert LX <= 3 and LY <= 4 and EZ <= 8 and n_grp <= 2

        def reach(steps, local, count):
            return min(-(-steps // local), count - 1)

        RG, RH = reach(REACH, LX, n_gx), reach(REACH, LY, n_yz)
        RGF, RHF = reach(REACH_FACE, LX, n_gx), reach(REACH_FACE, LY, n_yz)
        WG = n_gx if n_gx <= 2 * RG + 1 else 2 * RG + 1
        WH = n_yz if n_yz <= 2 * RH + 1 else 2 * RH + 1
        cfg = (n_grp, n_gx, n_yz, LX, LY, LZ, WG, WH, RG, RH, RGF, RHF)
        spec = (P("gx", "yz", "grp", None), P("gx", "yz", "grp"), P("gx", "yz", "grp"), P(), P())
        run = jax.shard_map(
            functools.partial(body, cfg), mesh=mesh, in_specs=spec,
            out_specs=P("gx", "yz", "grp", None), check_vma=False,
        )
        return run(rhs, coeff, flags, basis, eigenvalues)

    return call
```

time: 232 us -> 23.2 us (0.10)
  the two profiles are of different devices: /device:TPU:26 before, /device:TPU:0 now
where the time goes in v1:
time: 23.2 us; the launch traced here: 23 us
  Pallas kernels  18.7 us (81%)
  local copies, waits for them, and re-layouts  4.28 us (18%)
    pallas_call x1, Pallas kernels, body(): pl.pallas_call(functools.partial(kernel, cfg), out_shape=jax.ShapeDtypeSt...  18.7 us
    unnamed x10, local copies, waits for them, and re-layouts  3.62 us
    reshape x1, local copies, waits for them, and re-layouts, body(): return out.reshape(rhs.shape)  0.67 us

profile of v1, /device:TPU:0, one launch (start us, length us, event | category | flops | bytes accessed | tf_op | source)
XLA Modules:
  0.0 23.0 jit_solution(5568248932589986929)
XLA Ops:
  0.0 0.0 copy-start.4
  0.0 0.7 %copy-done.4 = f32[8]{0:T(128)S(1)} copy-done((f32[8]{0:T(128)S(1)}, f32[8]{0:T(128)}, u32[]{:S(2)}) %copy-start.4) | copy-done | bytes 56
  0.7 0.0 copy-start
  0.7 0.9 %copy-done = f32[3,4,4,512]{3,2,1,0:T(4,128)S(1)} copy-done((f32[3,4,4,512]{3,2,1,0:T(4,128)S(1)}, f32[3,4,4,512]{3,2,1,0:T(4,128)}, u32[]{:S(2)}) %copy-start) | copy-done | bytes 98328
  1.5 0.0 copy-start.1
  1.6 0.7 %copy-done.1 = f32[3,4,4]{2,1,0:T(4,128)S(1)} copy-done((f32[3,4,4]{2,1,0:T(4,128)S(1)}, f32[3,4,4]{2,1,0:T(4,128)}, u32[]{:S(2)}) %copy-start.1) | copy-done | bytes 216
  2.2 0.0 copy-start.2
  2.2 0.7 %copy-done.2 = s32[3,4,4]{2,1,0:T(4,128)S(1)} copy-done((s32[3,4,4]{2,1,0:T(4,128)S(1)}, s32[3,4,4]{2,1,0:T(4,128)}, u32[]{:S(2)}) %copy-start.2) | copy-done | bytes 216
  2.9 0.0 copy-start.3
  2.9 0.7 %copy-done.3 = f32[8,8]{1,0:T(8,128)S(1)} copy-done((f32[8,8]{1,0:T(8,128)S(1)}, f32[8,8]{1,0:T(8,128)}, u32[]{:S(2)}) %copy-start.3) | copy-done | bytes 280
  3.6 18.7 %shard_map.55 = f32[48,512]{1,0:T(8,128)S(1)} custom-call(f32[3,4,4,512]{3,2,1,0:T(4,128)S(1)} %copy-done, f32[3,4,4]{2,1,0:T(4,128)S(1)} %copy-done.1, s32[3,4,4]{2,1,0:T(4,128)S(1)} %copy-done.2, f32[8,8]{1,0:T(8,128)S(1)} %copy-done.3, f32[1,8]{1,0:T(1,128)S(1)} %bitcast.1), custom_call_target="tpu_custom_call" | custom-call | tf_op jit(solution)/shard_map/pallas_call | solution.py:480
  22.3 0.7 %reshape.7 = f32[3,4,4,512]{3,2,1,0:T(4,128)} reshape(f32[48,512]{1,0:T(8,128)S(1)} %shard_map.55) | data formatting | bytes 196608 | tf_op jit(solution)/shard_map/reshape | solution.py:514
Async XLA Ops:
  0.0 0.7 %copy-start.4 = (f32[8]{0:T(128)S(1)}, f32[8]{0:T(128)}, u32[]{:S(2)}) copy-start(f32[8]{0:T(128)} %param.9) | copy-start | bytes 100
  0.7 0.9 %copy-start = (f32[3,4,4,512]{3,2,1,0:T(4,128)S(1)}, f32[3,4,4,512]{3,2,1,0:T(4,128)}, u32[]{:S(2)}) copy-start(f32[3,4,4,512]{3,2,1,0:T(4,128)} %rhs_ref.1) | copy-start | bytes 294916
  1.5 0.7 %copy-start.1 = (f32[3,4,4]{2,1,0:T(4,128)S(1)}, f32[3,4,4]{2,1,0:T(4,128)}, u32[]{:S(2)}) copy-start(f32[3,4,4]{2,1,0:T(4,128)} %coeff_ref.1) | copy-start | bytes 580
  2.2 0.7 %copy-start.2 = (s32[3,4,4]{2,1,0:T(4,128)S(1)}, s32[3,4,4]{2,1,0:T(4,128)}, u32[]{:S(2)}) copy-start(s32[3,4,4]{2,1,0:T(4,128)} %flags_ref.1) | copy-start | bytes 580
  2.9 0.7 %copy-start.3 = (f32[8,8]{1,0:T(8,128)S(1)}, f32[8,8]{1,0:T(8,128)}, u32[]{:S(2)}) copy-start(f32[8,8]{1,0:T(8,128)} %basis_ref.1) | copy-start | bytes 772

commit v2 on v1

--- a/solution.py
+++ b/solution.py
@@ -61,20 +61,17 @@
     return out
 
 
-def offsets(reach):
-    return [k for r in range(1, reach + 1) for k in (-r, r)]
-
-
 def kernel(
     cfg,
+    rhs_hbm, coeff_hbm, flags_hbm, basis_hbm, eig_hbm,
+    out_ref,
     rhs_ref, coeff_ref, flags_ref, basis_ref, eig_ref,
-    out_ref,
-    mine, other, win, planes, cfx, ext3, ext1,
+    mine_b, other_b, mine_p, other_p, win_b, win_p, planes, cfx, ext3, ext1,
     rhs_s, s_ref, e_hi, e_lo, t_hi, t_lo,
     ysend, yrecv, zsend, zrecv, xrecv, nb,
-    send_sem, recv_sem, fsend, frecv,
+    in_sem, b_send, b_recv, p_send, p_recv, g_send, g_recv, fsend, frecv,
 ):
-    n_grp, n_gx, n_yz, LX, LY, LZ, WG, WH, RG, RH, RGF, RHF = cfg
+    n_grp, n_gx, n_yz, LX, LY, LZ, WG, WH, RG, RH = cfg
     LT = planes.shape[0]
     L = LT * 128
     XP = cfx.shape[1]
@@ -89,9 +86,17 @@
     g_start = 0 if full_g else me_gx - RG
     h_start = 0 if full_h else me_yz - RH
 
-    win[...] = jnp.zeros(win.shape, F32)
-    planes[...] = jnp.zeros(planes.shape, F32)
-    cfx[...] = jnp.zeros(cfx.shape, F32)
+    loads = []
+    pairs_in = [
+        (basis_hbm, basis_ref), (eig_hbm, eig_ref), (rhs_hbm, rhs_ref),
+        (coeff_hbm, coeff_ref), (flags_hbm, flags_ref),
+    ]
+    for n, (src, dst) in enumerate(pairs_in):
+        load = pltpu.make_async_copy(src, dst, in_sem.at[n])
+        load.start()
+        loads.append(load)
+    win_b[...] = jnp.zeros(win_b.shape, F32)
+    win_p[...] = jnp.zeros(win_p.shape, F32)
 
     me_of = {"grp": me_grp, "gx": me_gx, "yz": me_yz}
     n_of = {"grp": n_grp, "gx": n_gx, "yz": n_yz}
@@ -100,26 +105,77 @@
         at = me_of[axis] + k
         return jnp.logical_and(at >= 0, at < n_of[axis])
 
-    peers = [("grp", k) for k in offsets(min(1, n_grp - 1))]
-    peers += [("gx", k) for k in offsets(RG)]
-    peers += [("yz", k) for k in offsets(RH)]
+    def cost(k, local):
+        return 0 if k == 0 else (abs(k) - 1) * local + 1
+
+    def around(reach):
+        return [
+            (kg, kh)
+            for kg in range(-RG, RG + 1)
+            for kh in range(-RH, RH + 1)
+            if (kg, kh) != (0, 0) and cost(kg, LX) + cost(kh, LY) <= reach
+        ]
+
+    def target(key):
+        return {axis: me_of[axis] + k for axis, k in key if k}
+
+    def present(key):
+        there = None
+        for axis, k in key:
+            if k:
+                here = exists(axis, k)
+                there = here if there is None else jnp.logical_and(there, here)
+        return there
+
+    grp_keys = [(("grp", k),) for k in (-1, 1)] if n_grp > 1 else []
+    b_keys = [(("gx", kg), ("yz", kh)) for kg, kh in around(REACH)]
+    p_keys = [(("gx", kg), ("yz", kh)) for kg, kh in around(REACH_FACE)]
 
     barrier = pltpu.get_barrier_semaphore()
     count = jnp.int32(0)
-    for axis, k in peers:
-        here = exists(axis, k)
+    for key in grp_keys + b_keys:
+        here = present(key)
         count = count + here.astype(jnp.int32)
 
         @pl.when(here)
-        def _(axis=axis, k=k):
-            pl.semaphore_signal(barrier, inc=1, device_id={axis: me_of[axis] + k}, device_id_type=MESH)
-
-    basis = basis_ref[...]
+        def _(key=key):
+            pl.semaphore_signal(barrier, inc=1, device_id=target(key), device_id_type=MESH)
+
     lane = iota((8, NODES), 1)
     sub = iota((8, NODES), 0)
     v1 = (lane // 64 == sub).astype(F32)
     v2 = ((lane // 8) % 8 == sub).astype(F32)
     v3 = (lane % 8 == sub).astype(F32)
+
+    node_at = (lane // 64, (lane // 8) % 8, lane % 8)
+    side_at = (sub // 4, (sub // 2) % 2, sub % 2)
+    restrict = jnp.ones((8, NODES), F32)
+    for d in range(3):
+        restrict = restrict * jnp.where(side_at[d] == 0, pick(node_at[d], L0), pick(node_at[d], L1))
+    on_face = [
+        jnp.where(node_at[d] == 7 * side_at[d], restrict, 0.0) for d in range(3)
+    ]
+    faces = jnp.concatenate(on_face, axis=0)
+
+    YZ = LY * LZ
+    NE = LX * YZ
+    row = iota((NE, 1), 0)
+    row_x, row_y, row_z = row // YZ, (row // LZ) % LY, row % LZ
+    ysel = (iota((YZ, LY), 0) // LZ == iota((YZ, LY), 1)).astype(F32)
+    zsel = iota((YZ, LZ), 0) % LZ == iota((YZ, LZ), 1)
+
+    r16 = iota((YZ, 128), 0)
+    l16 = iota((YZ, 128), 1)
+    spot = (r16 // LZ) * 8 + me_grp * LZ + r16 % LZ
+    tail = (l16 == 96 + spot).astype(F32)
+    re = iota((NE, 128), 0)
+    place = (
+        iota((NE, 128), 1) == (re // YZ) * 32 + ((re // LZ) % LY) * 8 + me_grp * LZ + re % LZ
+    ).astype(F32)
+
+    loads[0].wait()
+    loads[1].wait()
+    basis = basis_ref[...]
 
     def build(hi_ref, lo_ref, dims):
         t1 = dot(basis, v1, dims)
@@ -135,28 +191,13 @@
     build(t_hi, t_lo, ((0,), (0,)))
     spectrum = dot(eig_ref[...], v1 + v2 + v3)
 
-    node_at = (lane // 64, (lane // 8) % 8, lane % 8)
-    side_at = (sub // 4, (sub // 2) % 2, sub % 2)
-    restrict = jnp.ones((8, NODES), F32)
-    for d in range(3):
-        restrict = restrict * jnp.where(side_at[d] == 0, pick(node_at[d], L0), pick(node_at[d], L1))
-    on_face = [
-        jnp.where(node_at[d] == 7 * side_at[d], restrict, 0.0) for d in range(3)
-    ]
-    faces = jnp.concatenate(on_face, axis=0)
-
-    YZ = LY * LZ
-    NE = LX * YZ
+    for load in loads[2:]:
+        load.wait()
     for x in range(LX):
         for y in range(LY):
             at = x * YZ + y * LZ
             rhs_s[at : at + LZ, :] = rhs_ref[x, y]
     rhs = rhs_s[...]
-    row = iota((NE, 1), 0)
-    row_x, row_y, row_z = row // YZ, (row // LZ) % LY, row % LZ
-    ysel = (iota((YZ, LY), 0) // LZ == iota((YZ, LY), 1)).astype(F32)
-    zsel = iota((YZ, LZ), 0) % LZ == iota((YZ, LZ), 1)
-
     def column(ref):
         parts = []
         for x in range(LX):
@@ -170,25 +211,61 @@
     flag_col = jnp.concatenate(flag_cols, axis=0)
     inverse = 1.0 / (coeff_col * spectrum)
 
-    r16 = iota((YZ, 128), 0)
-    l16 = iota((YZ, 128), 1)
-    spot = (r16 // LZ) * 8 + me_grp * LZ + r16 % LZ
-    tail = (l16 == 96 + spot).astype(F32)
-    re = iota((NE, 128), 0)
-    place = (
-        iota((NE, 128), 1) == (re // YZ) * 32 + ((re // LZ) % LY) * 8 + me_grp * LZ + re % LZ
-    ).astype(F32)
-
     b_own = dot(dot(restrict, rhs, ((1,), (1,))), place)
     row8 = iota((8, 128), 0)
     for x in range(LX):
         c_line = jnp.sum(coeff_cols[x] * tail, axis=0, keepdims=True)
         f_line = jnp.sum(flag_cols[x] * tail, axis=0, keepdims=True)
         b_own = b_own + jnp.where(row8 == x, c_line, 0.0) + jnp.where(row8 == LX + x, f_line, 0.0)
+    mine_b[...] = b_own
+
+    def remote(src, dst, send, recv, n, key):
+        copy = pltpu.make_async_remote_copy(
+            src_ref=src, dst_ref=dst, send_sem=send.at[n], recv_sem=recv.at[n],
+            device_id=target(key), device_id_type=MESH,
+        )
+        return key, copy
+
+    def around_copies(ref, keys, send, recv):
+        found = []
+        for n, key in enumerate(keys):
+            kg, kh = key[0][1], key[1][1]
+            slot = (hs if full_h else RH - kh, gs if full_g else RG - kg)
+            found.append(remote(ref.at[hs, gs], ref.at[slot[0], slot[1]], send, recv, n, key))
+        return found
+
+    def start_all(copies):
+        for key, copy in copies:
+            @pl.when(present(key))
+            def _(copy=copy):
+                copy.start()
+
+    def wait_recv(copies):
+        for key, copy in copies:
+            @pl.when(present([(axis, -k) for axis, k in key]))
+            def _(copy=copy):
+                copy.wait_recv()
+
+    def wait_send(copies):
+        for key, copy in copies:
+            @pl.when(present(key))
+            def _(copy=copy):
+                copy.wait_send()
+
+    grp_b = [remote(mine_b, other_b, g_send, g_recv, n, key) for n, key in enumerate(grp_keys)]
+    grp_p = [remote(mine_p, other_p, g_send, g_recv, 2 + n, key) for n, key in enumerate(grp_keys)]
+    all_b = around_copies(win_b, b_keys, b_send, b_recv)
+    all_p = around_copies(win_p, p_keys, p_send, p_recv)
+
+    pl.semaphore_wait(barrier, count)
+    start_all(grp_b)
     s = dot3(dot3(rhs, e_hi[...], e_lo[...]) * inverse, t_hi[...], t_lo[...])
     s_ref[...] = s
-    mine[0:8, :] = b_own
-    mine[8:32, :] = dot(dot(faces, s, ((1,), (1,))), place)
+    wait_recv(grp_b)
+    win_b[hs, gs] = mine_b[...] + other_b[...] if n_grp > 1 else mine_b[...]
+    start_all(all_b)
+    mine_p[...] = dot(dot(faces, s, ((1,), (1,))), place)
+    start_all(grp_p)
 
     for side in range(2):
         yy, zz = (0, 0) if side == 0 else (LY - 1, LZ - 1)
@@ -213,73 +290,16 @@
                 src, dst = ysend.at[side], yrecv.at[1 - side]
             else:
                 src, dst = zsend.at[side], zrecv.at[1 - side]
-            copy = pltpu.make_async_remote_copy(
-                src_ref=src, dst_ref=dst, send_sem=fsend.at[n], recv_sem=frecv.at[n],
-                device_id={axis: me_of[axis] + k}, device_id_type=MESH,
-            )
-            found.append((axis, k, copy))
+            found.append(remote(src, dst, fsend, frecv, n, ((axis, k),)))
         return found
 
-    def phase_copies(axis):
-        found = []
-        for axis_p, k in peers:
-            n = peers.index((axis_p, k))
-            if axis_p != axis:
-                continue
-            if axis == "grp":
-                src, dst = mine, other
-            elif axis == "gx":
-                src, dst = win.at[hs, gs], win.at[hs, gs if full_g else RG - k]
-                if abs(k) > RGF:
-                    src, dst = src.at[pl.ds(0, 8)], dst.at[pl.ds(0, 8)]
-            else:
-                src, dst = win.at[hs], win.at[hs if full_h else RH - k]
-                if abs(k) > RHF:
-                    src, dst = src.at[:, pl.ds(0, 8)], dst.at[:, pl.ds(0, 8)]
-            copy = pltpu.make_async_remote_copy(
-                src_ref=src, dst_ref=dst, send_sem=send_sem.at[n], recv_sem=recv_sem.at[n],
-                device_id={axis: me_of[axis] + k}, device_id_type=MESH,
-            )
-            found.append((axis, k, copy))
-        return found
-
-    def recv_of(axis, k, copy_list):
-        return next(c for a, j, c in copy_list if (a, j) == (axis, k))
-
-    def start_all(copies):
-        for axis, k, copy in copies:
-            @pl.when(exists(axis, k))
-            def _(copy=copy):
-                copy.start()
-
-    def wait_recv(copies):
-        for axis, k, copy in copies:
-            @pl.when(exists(axis, -k))
-            def _(copy=copy):
-                copy.wait_recv()
-
-    def wait_send(copies):
-        for axis, k, copy in copies:
-            @pl.when(exists(axis, k))
-            def _(copy=copy):
-                copy.wait_send()
-
-    pl.semaphore_wait(barrier, count)
-
-    grp_copies = phase_copies("grp")
-    gx_copies = phase_copies("gx")
-    yz_copies = phase_copies("yz")
     next_door = face_copies()
-    start_all(grp_copies)
-    wait_recv(grp_copies)
-    if n_grp > 1:
-        win[hs, gs] = mine[...] + other[...]
-    else:
-        win[hs, gs] = mine[...]
-    start_all(gx_copies)
     start_all(next_door)
-    wait_recv(gx_copies)
-    start_all(yz_copies)
+    wait_recv(grp_p)
+    win_p[hs, gs] = mine_p[...] + other_p[...] if n_grp > 1 else mine_p[...]
+    start_all(all_p)
+    planes[...] = jnp.zeros(planes.shape, F32)
+    cfx[...] = jnp.zeros(cfx.shape, F32)
     wait_recv(next_door)
 
     own_at = (me_gx * LX + row_x, me_yz * LY + row_y, me_grp * LZ + row_z)
@@ -314,32 +334,38 @@
             term = gain * s - jnp.where(has, moved, 0.0)
             face_s = face_s + jnp.where(node_of[d] == 7 * side, term, 0.0)
 
-    wait_recv(yz_copies)
-
-    lane_slot = iota((32, L), 1) // 32
-    for g in range(WG):
-        cf_plane = jnp.zeros((8, L), F32)
-        tiles = []
-        for h in range(WH):
-            tile = win[h, g]
-            if L > 128:
-                tile = jnp.concatenate([tile, jnp.zeros((32, L - 128), F32)], axis=1)
-            tiles.append(tile)
-            moved = pltpu.roll(tile[0:8], (32 * (h - 3)) % L, 1)
-            cf_plane = jnp.where(lane_slot[0:8] == h, moved, cf_plane)
-        for x in range(LX):
-            plane = jnp.zeros((32, L), F32)
+    wait_recv(all_b)
+
+    def spread(win, rows, first_field):
+        lane_slot = iota((rows, L), 1) // 32
+        for g in range(WG):
+            cf_plane = jnp.zeros((rows, L), F32)
+            tiles = []
             for h in range(WH):
-                amount = (32 * (h - x)) % L
-                moved = pltpu.roll(tiles[h], amount, 1) if amount else tiles[h]
-                plane = jnp.where(lane_slot == h, moved, plane)
-            at = (g * LX + x) * 8
-            for f in range(4):
-                for t in range(LT):
-                    part = plane[f * 8 : f * 8 + 8, t * 128 : (t + 1) * 128]
-                    planes[t, f * FROWS + at : f * FROWS + at + 8, :] = part
-        cfx[0, g * LX : (g + 1) * LX, :] = cf_plane[0:LX]
-        cfx[1, g * LX : (g + 1) * LX, :] = cf_plane[LX : 2 * LX]
+                tile = win[h, g]
+                if L > 128:
+                    tile = jnp.concatenate([tile, jnp.zeros((rows, L - 128), F32)], axis=1)
+                tiles.append(tile)
+                if first_field == 0:
+                    moved = pltpu.roll(tile, (32 * (h - 3)) % L, 1)
+                    cf_plane = jnp.where(lane_slot == h, moved, cf_plane)
+            for x in range(LX):
+                plane = jnp.zeros((rows, L), F32)
+                for h in range(WH):
+                    amount = (32 * (h - x)) % L
+                    moved = pltpu.roll(tiles[h], amount, 1) if amount else tiles[h]
+                    plane = jnp.where(lane_slot == h, moved, plane)
+                at = (g * LX + x) * 8
+                for f in range(rows // 8):
+                    to = (first_field + f) * FROWS + at
+                    for t in range(LT):
+                        part = plane[f * 8 : f * 8 + 8, t * 128 : (t + 1) * 128]
+                        planes[t, to : to + 8, :] = part
+            if first_field == 0:
+                cfx[0, g * LX : (g + 1) * LX, :] = cf_plane[0:LX]
+                cfx[1, g * LX : (g + 1) * LX, :] = cf_plane[LX : 2 * LX]
+
+    spread(win_b, 8, 0)
 
     def strided(ref, start, stride):
         parts = [ref[t, pl.ds(start, XP, stride=stride), :] for t in range(LT)]
@@ -353,7 +379,6 @@
         return [strided(planes, f * FROWS + a, 8) for a in range(8)]
 
     rhs1 = field(0)
-    proj = [field(1 + d) for d in range(3)]
     coeff = cfx[0]
     flag = cfx[1]
     pos = (
@@ -434,10 +459,6 @@
             q = side_of(a, d)
             inner = inner + stiff[q][q] * masses[d][a] + stiff[q][1 - q] * masses[d][a ^ bit[d]]
         rhs2.append(0.5 * rhs1[a] - 0.5 * coeff * inner)
-    for d in range(3):
-        both = [proj[d][a] + masses[d][a] for a in range(8)]
-        rhs2 = [rhs2[a] - jump(both, a, d) for a in range(8)]
-
     first_row = gs * LX
     absolute = hs * 32 + (iota((YZ, L), 0) // LZ) * 8 + me_grp * LZ + iota((YZ, L), 0) % LZ
     take = (iota((YZ, L), 1) == absolute).astype(F32)
@@ -460,32 +481,46 @@
     total = face_s + face_c
     smooth2 = dot3(dot3(total, e_hi[...], e_lo[...]) * inverse, t_hi[...], t_lo[...])
 
+    wait_recv(all_p)
+    spread(win_p, 24, 1)
+    proj = [field(1 + d) for d in range(3)]
+    for d in range(3):
+        both = [proj[d][a] + masses[d][a] for a in range(8)]
+        rhs2 = [rhs2[a] - jump(both, a, d) for a in range(8)]
     c2 = cheb(rhs2)
     for a in range(8):
         store_strided(ext1, a, 8, 0.25 * c1[a] + 0.5 * c2[a])
     lifted = dot(own_values(ext1, 8), restrict)
     out_ref[...] = 0.75 * s + lifted - 0.5 * smooth2
 
-    for copies in (grp_copies, gx_copies, yz_copies, next_door):
+    for copies in (grp_b, grp_p, all_b, all_p, next_door):
         wait_send(copies)
 
 
 def body(cfg, rhs, coeff, flags, basis, eigenvalues):
-    n_grp, n_gx, n_yz, LX, LY, LZ, WG, WH, RG, RH, RGF, RHF = cfg
+    n_grp, n_gx, n_yz, LX, LY, LZ, WG, WH, RG, RH = cfg
     NE = LX * LY * LZ
     L = -(-(WH * 32) // 128) * 128
     XP = -(-(WG * LX) // 8) * 8
     V = pltpu.VMEM
-    n_peers = 2 * (1 + RG + RH)
+    n_peers = (2 * RG + 1) * (2 * RH + 1)
     out = pl.pallas_call(
         functools.partial(kernel, cfg),
         out_shape=jax.ShapeDtypeStruct((NE, NODES), F32),
-        in_specs=[pl.BlockSpec(memory_space=V)] * 5,
+        in_specs=[pl.BlockSpec(memory_space=pltpu.HBM)] * 5,
         out_specs=pl.BlockSpec(memory_space=V),
         scratch_shapes=[
-            V((32, 128), F32),
-            V((32, 128), F32),
-            V((WH, WG, 32, 128), F32),
+            V(rhs.shape, F32),
+            V(coeff.shape, F32),
+            V(flags.shape, jnp.int32),
+            V(basis.shape, F32),
+            V((1, DEG1), F32),
+            V((8, 128), F32),
+            V((8, 128), F32),
+            V((24, 128), F32),
+            V((24, 128), F32),
+            V((WH, WG, 8, 128), F32),
+            V((WH, WG, 24, 128), F32),
             V((L // 128, 4 * XP * 8, 128), F32),
             V((2, XP, L), F32),
             V((L // 128, XP * 24, 128), F32),
@@ -502,13 +537,18 @@
             V((2, 16, NODES), F32),
             V((2, LY * LZ, NODES), F32),
             V((NE, NODES), F32),
+            pltpu.SemaphoreType.DMA((5,)),
             pltpu.SemaphoreType.DMA((n_peers,)),
             pltpu.SemaphoreType.DMA((n_peers,)),
+            pltpu.SemaphoreType.DMA((n_peers,)),
+            pltpu.SemaphoreType.DMA((n_peers,)),
+            pltpu.SemaphoreType.DMA((4,)),
+            pltpu.SemaphoreType.DMA((4,)),
             pltpu.SemaphoreType.DMA((6,)),
             pltpu.SemaphoreType.DMA((6,)),
         ],
         compiler_params=pltpu.CompilerParams(
-            collective_id=0, has_side_effects=True, vmem_limit_bytes=32 * 1024 * 1024
+            collective_id=0, has_side_effects=True, vmem_limit_bytes=60 * 1024 * 1024
         ),
     )(rhs, coeff, flags, basis, eigenvalues.reshape(1, DEG1))
     return out.reshape(rhs.shape)
@@ -526,10 +566,9 @@
             return min(-(-steps // local), count - 1)
 
         RG, RH = reach(REACH, LX, n_gx), reach(REACH, LY, n_yz)
-        RGF, RHF = reach(REACH_FACE, LX, n_gx), reach(REACH_FACE, LY, n_yz)
         WG = n_gx if n_gx <= 2 * RG + 1 else 2 * RG + 1
         WH = n_yz if n_yz <= 2 * RH + 1 else 2 * RH + 1
-        cfg = (n_grp, n_gx, n_yz, LX, LY, LZ, WG, WH, RG, RH, RGF, RHF)
+        cfg = (n_grp, n_gx, n_yz, LX, LY, LZ, WG, WH, RG, RH)
         spec = (P("gx", "yz", "grp", None), P("gx", "yz", "grp"), P("gx", "yz", "grp"), P(), P())
         run = jax.shard_map(
             functools.partial(body, cfg), mesh=mesh, in_specs=spec,

time: 23.2 us -> 18.8 us (0.81)
  local copies, waits for them, and re-layouts: 4.28 us -> 1.56 us
  Pallas kernels: 18.7 us -> 17.1 us
    unnamed x10 -> x0, local copies, waits for them, and re-layouts: 3.62 us -> none
    pallas_call x1, Pallas kernels: 18.7 us -> 17.1 us  [body(): pl.pallas_call(functools.partial(kernel, cfg), out_shape=jax.ShapeDtypeSt...]
    reshape x1, local copies, waits for them, and re-layouts: 0.67 us -> 1.56 us  [body(): return out.reshape(rhs.shape)]
where the time goes in v2:
time: 18.8 us; the launch traced here: 18.7 us
  Pallas kernels  17.1 us (91%)
  local copies, waits for them, and re-layouts  1.56 us (8%)
    pallas_call x1, Pallas kernels, body(): pl.pallas_call(functools.partial(kernel, cfg), out_shape=jax.ShapeDtypeSt...  17.1 us
    reshape x1, local copies, waits for them, and re-layouts, body(): return out.reshape(rhs.shape)  1.56 us

profile of v2, /device:TPU:0, one launch (start us, length us, event | category | flops | bytes accessed | tf_op | source)
XLA Modules:
  0.0 18.7 jit_solution(13015655362105017441)
XLA Ops:
  0.0 17.1 %shard_map.55 = f32[48,512]{1,0:T(8,128)} custom-call(f32[3,4,4,512]{3,2,1,0:T(4,128)} %rhs_hbm.1, f32[3,4,4]{2,1,0:T(4,128)} %coeff_hbm.1, s32[3,4,4]{2,1,0:T(4,128)} %flags_hbm.1, f32[8,8]{1,0:T(8,128)} %basis_hbm.1, f32[1,8]{1,0:T(1,128)} %bitcast.1), custom_call_target="tpu_custom_call" | custom-call | tf_op jit(solution)/shard_map/pallas_call | solution.py:507
  17.1 1.6 %reshape.7 = f32[3,4,4,512]{3,2,1,0:T(4,128)} reshape(f32[48,512]{1,0:T(8,128)} %shard_map.55) | data formatting | bytes 196608 | tf_op jit(solution)/shard_map/reshape | solution.py:554

commit v3 on v2

--- a/solution.py
+++ b/solution.py
@@ -29,7 +29,6 @@
 L1 = [(1.0 + x) * 0.5 for x in GLL_POINTS]
 MASS_SAME = sum(a * a for a in L0)
 MASS_OTHER = sum(a * b for a, b in zip(L0, L1))
-HIGHEST = lax.Precision.HIGHEST
 MESH = pl.DeviceIdType.MESH
 F32 = jnp.float32
 BF16 = jnp.bfloat16
@@ -39,8 +38,25 @@
     return lax.broadcasted_iota(jnp.int32, shape, dim)
 
 
-def dot(a, b, dims=((1,), (0,))):
-    return lax.dot_general(a, b, (dims, ((), ())), precision=HIGHEST, preferred_element_type=F32)
+def parts_of(x, count):
+    found = []
+    for _ in range(count):
+        head = x.astype(BF16)
+        found.append(head)
+        x = x - head.astype(F32)
+    return found
+
+
+def dot(a, b, dims=((1,), (0,)), parts=(2, 2)):
+    pa, pb = parts_of(a, parts[0]), parts_of(b, parts[1])
+    order = max(parts)
+    out = None
+    for p in range(parts[0]):
+        for q in range(parts[1]):
+            if p + q < order:
+                term = lax.dot_general(pa[p], pb[q], (dims, ((), ())), preferred_element_type=F32)
+                out = term if out is None else out + term
+    return out
 
 
 def split(x):
@@ -50,8 +66,9 @@
 
 def dot3(x, hi, lo):
     xh, xl = split(x)
-    d = functools.partial(jnp.dot, preferred_element_type=F32)
-    return d(xh, hi) + (d(xl, hi) + d(xh, lo))
+    rows = x.shape[0]
+    both = jnp.dot(jnp.concatenate([xh, xl], axis=0), hi, preferred_element_type=F32)
+    return both[:rows] + (both[rows:] + jnp.dot(xh, lo, preferred_element_type=F32))
 
 
 def pick(index, table):
@@ -173,24 +190,6 @@
         iota((NE, 128), 1) == (re // YZ) * 32 + ((re // LZ) % LY) * 8 + me_grp * LZ + re % LZ
     ).astype(F32)
 
-    loads[0].wait()
-    loads[1].wait()
-    basis = basis_ref[...]
-
-    def build(hi_ref, lo_ref, dims):
-        t1 = dot(basis, v1, dims)
-        t2 = dot(basis, v2, dims)
-        t3 = dot(basis, v3, dims)
-        pairs = jnp.concatenate([t2[j : j + 1, :] * t3 for j in range(8)], axis=0)
-        for i in range(8):
-            hi, lo = split(t1[i : i + 1, :] * pairs)
-            hi_ref[i * 64 : (i + 1) * 64, :] = hi
-            lo_ref[i * 64 : (i + 1) * 64, :] = lo
-
-    build(e_hi, e_lo, ((1,), (0,)))
-    build(t_hi, t_lo, ((0,), (0,)))
-    spectrum = dot(eig_ref[...], v1 + v2 + v3)
-
     for load in loads[2:]:
         load.wait()
     for x in range(LX):
@@ -201,7 +200,7 @@
     def column(ref):
         parts = []
         for x in range(LX):
-            spread = dot(ysel, ref[x].astype(F32))
+            spread = dot(ysel, ref[x].astype(F32), parts=(1, 3))
             parts.append(jnp.sum(jnp.where(zsel, spread, 0.0), axis=1, keepdims=True))
         return parts
 
@@ -209,9 +208,8 @@
     flag_cols = column(flags_ref)
     coeff_col = jnp.concatenate(coeff_cols, axis=0)
     flag_col = jnp.concatenate(flag_cols, axis=0)
-    inverse = 1.0 / (coeff_col * spectrum)
-
-    b_own = dot(dot(restrict, rhs, ((1,), (1,))), place)
+
+    b_own = dot(dot(restrict, rhs, ((1,), (1,))), place, parts=(2, 1))
     row8 = iota((8, 128), 0)
     for x in range(LX):
         c_line = jnp.sum(coeff_cols[x] * tail, axis=0, keepdims=True)
@@ -259,12 +257,31 @@
 
     pl.semaphore_wait(barrier, count)
     start_all(grp_b)
+    loads[0].wait()
+    loads[1].wait()
+    basis = basis_ref[...]
+
+    def build(hi_ref, lo_ref, dims):
+        t1 = dot(basis, v1, dims, (3, 1))
+        t2 = dot(basis, v2, dims, (3, 1))
+        t3 = dot(basis, v3, dims, (3, 1))
+        pairs = jnp.concatenate([t2[j : j + 1, :] * t3 for j in range(8)], axis=0)
+        for i in range(8):
+            hi, lo = split(t1[i : i + 1, :] * pairs)
+            hi_ref[i * 64 : (i + 1) * 64, :] = hi
+            lo_ref[i * 64 : (i + 1) * 64, :] = lo
+
+    build(e_hi, e_lo, ((1,), (0,)))
+    build(t_hi, t_lo, ((0,), (0,)))
+    spectrum = dot(eig_ref[...], v1 + v2 + v3, parts=(3, 1))
+
+    inverse = 1.0 / (coeff_col * spectrum)
     s = dot3(dot3(rhs, e_hi[...], e_lo[...]) * inverse, t_hi[...], t_lo[...])
     s_ref[...] = s
     wait_recv(grp_b)
     win_b[hs, gs] = mine_b[...] + other_b[...] if n_grp > 1 else mine_b[...]
     start_all(all_b)
-    mine_p[...] = dot(dot(faces, s, ((1,), (1,))), place)
+    mine_p[...] = dot(dot(faces, s, ((1,), (1,))), place, parts=(2, 1))
     start_all(grp_p)
 
     for side in range(2):
@@ -470,7 +487,7 @@
             part = 0.0
             for t in range(LT):
                 lanes = take[:, t * 128 : (t + 1) * 128]
-                part = part + dot(lanes, ref[t, pl.ds(start, comps), :], ((1,), (1,)))
+                part = part + dot(lanes, ref[t, pl.ds(start, comps), :], ((1,), (1,)), (1, 2))
             parts.append(part)
         return jnp.concatenate(parts, axis=0)
 
@@ -506,7 +523,7 @@
     n_peers = (2 * RG + 1) * (2 * RH + 1)
     out = pl.pallas_call(
         functools.partial(kernel, cfg),
-        out_shape=jax.ShapeDtypeStruct((NE, NODES), F32),
+        out_shape=V((NE, NODES), F32),
         in_specs=[pl.BlockSpec(memory_space=pltpu.HBM)] * 5,
         out_specs=pl.BlockSpec(memory_space=V),
         scratch_shapes=[

time: 18.8 us -> 17.1 us (0.910)
  local copies, waits for them, and re-layouts: 1.56 us -> 0.67 us
  Pallas kernels: 17.1 us -> 16.3 us
    reshape x1, local copies, waits for them, and re-layouts: 1.56 us -> 0.67 us  [body(): return out.reshape(rhs.shape)]
    pallas_call x1, Pallas kernels: 17.1 us -> 16.3 us  [body(): pl.pallas_call(functools.partial(kernel, cfg), out_shape=V((NE, NODES), F...]
where the time goes in v3:
time: 17.1 us; the launch traced here: 17 us
  Pallas kernels  16.3 us (95%)
  local copies, waits for them, and re-layouts  0.67 us (4%)
    pallas_call x1, Pallas kernels, body(): pl.pallas_call(functools.partial(kernel, cfg), out_shape=V((NE, NODES), F...  16.3 us
    reshape x1, local copies, waits for them, and re-layouts, body(): return out.reshape(rhs.shape)  0.67 us

profile of v3, /device:TPU:0, one launch (start us, length us, event | category | flops | bytes accessed | tf_op | source)
XLA Modules:
  0.0 17.0 jit_solution(17356864474474710410)
XLA Ops:
  0.0 16.3 %shard_map.55 = f32[48,512]{1,0:T(8,128)S(1)} custom-call(f32[3,4,4,512]{3,2,1,0:T(4,128)} %rhs_hbm.1, f32[3,4,4]{2,1,0:T(4,128)} %coeff_hbm.1, s32[3,4,4]{2,1,0:T(4,128)} %flags_hbm.1, f32[8,8]{1,0:T(8,128)} %basis_hbm.1, f32[1,8]{1,0:T(1,128)} %bitcast.1), custom_call_target="tpu_custom_call" | custom-call | tf_op jit(solution)/shard_map/pallas_call | solution.py:524
  16.3 0.7 %reshape.7 = f32[3,4,4,512]{3,2,1,0:T(4,128)} reshape(f32[48,512]{1,0:T(8,128)S(1)} %shard_map.55) | data formatting | bytes 196608 | tf_op jit(solution)/shard_map/reshape | solution.py:571

commit v4 on v3

--- a/solution.py
+++ b/solution.py
@@ -145,12 +145,14 @@
         return there
 
     grp_keys = [(("grp", k),) for k in (-1, 1)] if n_grp > 1 else []
-    b_keys = [(("gx", kg), ("yz", kh)) for kg, kh in around(REACH)]
+    gx_keys = [(("gx", k),) for k in range(-RG, RG + 1) if k]
+    yz_keys = [(("yz", k),) for k in range(-RH, RH + 1) if k]
     p_keys = [(("gx", kg), ("yz", kh)) for kg, kh in around(REACH_FACE)]
 
     barrier = pltpu.get_barrier_semaphore()
     count = jnp.int32(0)
-    for key in grp_keys + b_keys:
+    diagonal = [key for key in p_keys if key[0][1] and key[1][1]]
+    for key in grp_keys + gx_keys + yz_keys + diagonal:
         here = present(key)
         count = count + here.astype(jnp.int32)
 
@@ -252,7 +254,13 @@
 
     grp_b = [remote(mine_b, other_b, g_send, g_recv, n, key) for n, key in enumerate(grp_keys)]
     grp_p = [remote(mine_p, other_p, g_send, g_recv, 2 + n, key) for n, key in enumerate(grp_keys)]
-    all_b = around_copies(win_b, b_keys, b_send, b_recv)
+    gx_b, yz_b = [], []
+    for n, key in enumerate(gx_keys):
+        slot = gs if full_g else RG - key[0][1]
+        gx_b.append(remote(win_b.at[hs, gs], win_b.at[hs, slot], b_send, b_recv, n, key))
+    for n, key in enumerate(yz_keys):
+        slot = hs if full_h else RH - key[0][1]
+        yz_b.append(remote(win_b.at[hs], win_b.at[slot], b_send, b_recv, len(gx_keys) + n, key))
     all_p = around_copies(win_p, p_keys, p_send, p_recv)
 
     pl.semaphore_wait(barrier, count)
@@ -276,11 +284,14 @@
     spectrum = dot(eig_ref[...], v1 + v2 + v3, parts=(3, 1))
 
     inverse = 1.0 / (coeff_col * spectrum)
-    s = dot3(dot3(rhs, e_hi[...], e_lo[...]) * inverse, t_hi[...], t_lo[...])
-    s_ref[...] = s
     wait_recv(grp_b)
     win_b[hs, gs] = mine_b[...] + other_b[...] if n_grp > 1 else mine_b[...]
-    start_all(all_b)
+    start_all(gx_b)
+    inside = dot3(rhs, e_hi[...], e_lo[...])
+    wait_recv(gx_b)
+    start_all(yz_b)
+    s = dot3(inside * inverse, t_hi[...], t_lo[...])
+    s_ref[...] = s
     mine_p[...] = dot(dot(faces, s, ((1,), (1,))), place, parts=(2, 1))
     start_all(grp_p)
 
@@ -312,46 +323,9 @@
 
     next_door = face_copies()
     start_all(next_door)
-    wait_recv(grp_p)
-    win_p[hs, gs] = mine_p[...] + other_p[...] if n_grp > 1 else mine_p[...]
-    start_all(all_p)
     planes[...] = jnp.zeros(planes.shape, F32)
     cfx[...] = jnp.zeros(cfx.shape, F32)
-    wait_recv(next_door)
-
-    own_at = (me_gx * LX + row_x, me_yz * LY + row_y, me_grp * LZ + row_z)
-    totals = (n_gx * LX, n_yz * LY, n_grp * LZ)
-    node_lane = iota((1, NODES), 1)
-    node_of = (node_lane // 64, (node_lane // 8) % 8, node_lane % 8)
-    strides = (64, 8, 1)
-    face_s = jnp.zeros((NE, NODES), F32)
-    for d in range(3):
-        for side in range(2):
-            if d == 0:
-                if side == 0:
-                    beside = jnp.concatenate([xrecv[0], s[: NE - YZ]], axis=0)
-                else:
-                    beside = jnp.concatenate([s[YZ:], xrecv[1]], axis=0)
-            else:
-                step = LZ if d == 1 else 1
-                nb[...] = pltpu.roll(s, step if side == 0 else NE - step, 0)
-                for x in range(LX):
-                    if d == 1:
-                        at = x * YZ + (0 if side == 0 else (LY - 1) * LZ)
-                        nb[at : at + LZ, :] = yrecv[side, x * LZ : (x + 1) * LZ, :]
-                    else:
-                        for y in range(LY):
-                            at = x * YZ + y * LZ + (0 if side == 0 else LZ - 1)
-                            nb[at : at + 1, :] = zrecv[side, x * LY + y : x * LY + y + 1, :]
-                beside = nb[...]
-            has = own_at[d] > 0 if side == 0 else own_at[d] < totals[d] - 1
-            gain = jnp.where(has, 1.0, flag_col)
-            shift = 7 * strides[d]
-            moved = pltpu.roll(beside, NODES - shift if side == 0 else shift, 1)
-            term = gain * s - jnp.where(has, moved, 0.0)
-            face_s = face_s + jnp.where(node_of[d] == 7 * side, term, 0.0)
-
-    wait_recv(all_b)
+    wait_recv(yz_b)
 
     def spread(win, rows, first_field):
         lane_slot = iota((rows, L), 1) // 32
@@ -384,6 +358,8 @@
 
     spread(win_b, 8, 0)
 
+    totals = (n_gx * LX, n_yz * LY, n_grp * LZ)
+
     def strided(ref, start, stride):
         parts = [ref[t, pl.ds(start, XP, stride=stride), :] for t in range(LT)]
         return parts[0] if LT == 1 else jnp.concatenate(parts, axis=1)
@@ -464,6 +440,9 @@
         return [MASS_SAME * v[a] + MASS_OTHER * v[a ^ bit[d]] for a in range(8)]
 
     c1 = cheb(rhs1)
+    wait_recv(grp_p)
+    win_p[hs, gs] = mine_p[...] + other_p[...] if n_grp > 1 else mine_p[...]
+    start_all(all_p)
     m3 = mass(c1, 2)
     m23 = mass(m3, 1)
     m13 = mass(m3, 0)
@@ -476,6 +455,39 @@
             q = side_of(a, d)
             inner = inner + stiff[q][q] * masses[d][a] + stiff[q][1 - q] * masses[d][a ^ bit[d]]
         rhs2.append(0.5 * rhs1[a] - 0.5 * coeff * inner)
+    wait_recv(next_door)
+
+    own_at = (me_gx * LX + row_x, me_yz * LY + row_y, me_grp * LZ + row_z)
+    node_lane = iota((1, NODES), 1)
+    node_of = (node_lane // 64, (node_lane // 8) % 8, node_lane % 8)
+    strides = (64, 8, 1)
+    face_s = jnp.zeros((NE, NODES), F32)
+    for d in range(3):
+        for side in range(2):
+            if d == 0:
+                if side == 0:
+                    beside = jnp.concatenate([xrecv[0], s[: NE - YZ]], axis=0)
+                else:
+                    beside = jnp.concatenate([s[YZ:], xrecv[1]], axis=0)
+            else:
+                step = LZ if d == 1 else 1
+                nb[...] = pltpu.roll(s, step if side == 0 else NE - step, 0)
+                for x in range(LX):
+                    if d == 1:
+                        at = x * YZ + (0 if side == 0 else (LY - 1) * LZ)
+                        nb[at : at + LZ, :] = yrecv[side, x * LZ : (x + 1) * LZ, :]
+                    else:
+                        for y in range(LY):
+                            at = x * YZ + y * LZ + (0 if side == 0 else LZ - 1)
+                            nb[at : at + 1, :] = zrecv[side, x * LY + y : x * LY + y + 1, :]
+                beside = nb[...]
+            near = own_at[d] > 0 if side == 0 else own_at[d] < totals[d] - 1
+            factor = jnp.where(near, 1.0, flag_col)
+            shift = 7 * strides[d]
+            moved = pltpu.roll(beside, NODES - shift if side == 0 else shift, 1)
+            term = factor * s - jnp.where(near, moved, 0.0)
+            face_s = face_s + jnp.where(node_of[d] == 7 * side, term, 0.0)
+
     first_row = gs * LX
     absolute = hs * 32 + (iota((YZ, L), 0) // LZ) * 8 + me_grp * LZ + iota((YZ, L), 0) % LZ
     take = (iota((YZ, L), 1) == absolute).astype(F32)
@@ -510,7 +522,7 @@
     lifted = dot(own_values(ext1, 8), restrict)
     out_ref[...] = 0.75 * s + lifted - 0.5 * smooth2
 
-    for copies in (grp_b, grp_p, all_b, all_p, next_door):
+    for copies in (grp_b, gx_b, yz_b, grp_p, all_p, next_door):
         wait_send(copies)
 
 

time: 17.1 us -> 21.4 us (1.25)
  Pallas kernels: 16.3 us -> 20.6 us
    pallas_call x1, Pallas kernels: 16.3 us -> 20.6 us  [body(): pl.pallas_call(functools.partial(kernel, cfg), out_shape=V((NE, NODES), F...]
where the time goes in v4:
time: 21.4 us; the launch traced here: 21.3 us
  Pallas kernels  20.6 us (96%)
  local copies, waits for them, and re-layouts  0.67 us (3%)
    pallas_call x1, Pallas kernels, body(): pl.pallas_call(functools.partial(kernel, cfg), out_shape=V((NE, NODES), F...  20.6 us
    reshape x1, local copies, waits for them, and re-layouts, body(): return out.reshape(rhs.shape)  0.67 us

profile of v4, /device:TPU:0, one launch (start us, length us, event | category | flops | bytes accessed | tf_op | source)
XLA Modules:
  0.0 21.3 jit_solution(8371722739960618161)
XLA Ops:
  0.0 20.6 %shard_map.55 = f32[48,512]{1,0:T(8,128)S(1)} custom-call(f32[3,4,4,512]{3,2,1,0:T(4,128)} %rhs_hbm.1, f32[3,4,4]{2,1,0:T(4,128)} %coeff_hbm.1, s32[3,4,4]{2,1,0:T(4,128)} %flags_hbm.1, f32[8,8]{1,0:T(8,128)} %basis_hbm.1, f32[1,8]{1,0:T(1,128)} %bitcast.1), custom_call_target="tpu_custom_call" | custom-call | tf_op jit(solution)/shard_map/pallas_call | solution.py:536
  20.6 0.7 %reshape.7 = f32[3,4,4,512]{3,2,1,0:T(4,128)} reshape(f32[48,512]{1,0:T(8,128)S(1)} %shard_map.55) | data formatting | bytes 196608 | tf_op jit(solution)/shard_map/reshape | solution.py:583

commit v5 on v3

--- a/solution.py
+++ b/solution.py
@@ -276,11 +276,11 @@
     spectrum = dot(eig_ref[...], v1 + v2 + v3, parts=(3, 1))
 
     inverse = 1.0 / (coeff_col * spectrum)
-    s = dot3(dot3(rhs, e_hi[...], e_lo[...]) * inverse, t_hi[...], t_lo[...])
-    s_ref[...] = s
     wait_recv(grp_b)
     win_b[hs, gs] = mine_b[...] + other_b[...] if n_grp > 1 else mine_b[...]
     start_all(all_b)
+    s = dot3(dot3(rhs, e_hi[...], e_lo[...]) * inverse, t_hi[...], t_lo[...])
+    s_ref[...] = s
     mine_p[...] = dot(dot(faces, s, ((1,), (1,))), place, parts=(2, 1))
     start_all(grp_p)
 

time: 17.1 us -> 17.7 us (1.035)
  Pallas kernels: 16.3 us -> 16.9 us
    pallas_call x1, Pallas kernels: 16.3 us -> 16.9 us  [body(): pl.pallas_call(functools.partial(kernel, cfg), out_shape=V((NE, NODES), F...]
where the time goes in v5:
time: 17.7 us; the launch traced here: 17.5 us
  Pallas kernels  16.9 us (95%)
  local copies, waits for them, and re-layouts  0.67 us (4%)
    pallas_call x1, Pallas kernels, body(): pl.pallas_call(functools.partial(kernel, cfg), out_shape=V((NE, NODES), F...  16.9 us
    reshape x1, local copies, waits for them, and re-layouts, body(): return out.reshape(rhs.shape)  0.67 us

profile of v5, /device:TPU:0, one launch (start us, length us, event | category | flops | bytes accessed | tf_op | source)
XLA Modules:
  0.0 17.5 jit_solution(10917616954793474266)
XLA Ops:
  0.0 16.9 %shard_map.55 = f32[48,512]{1,0:T(8,128)S(1)} custom-call(f32[3,4,4,512]{3,2,1,0:T(4,128)} %rhs_hbm.1, f32[3,4,4]{2,1,0:T(4,128)} %coeff_hbm.1, s32[3,4,4]{2,1,0:T(4,128)} %flags_hbm.1, f32[8,8]{1,0:T(8,128)} %basis_hbm.1, f32[1,8]{1,0:T(1,128)} %bitcast.1), custom_call_target="tpu_custom_call" | custom-call | tf_op jit(solution)/shard_map/pallas_call | solution.py:524
  16.9 0.7 %reshape.7 = f32[3,4,4,512]{3,2,1,0:T(4,128)} reshape(f32[48,512]{1,0:T(8,128)S(1)} %shard_map.55) | data formatting | bytes 196608 | tf_op jit(solution)/shard_map/reshape | solution.py:571
